TPU v7x, 256 devices: a whole 4x4x8 slice. The times are simulated.
256 devices in a mesh: row: 32 (over z_hi, x, core), col: 8 (over y, z_lo).
Axes of the slice: x: 4, y: 4, z: 8 (z_hi: 4, z_lo: 2; z = z_hi * 2 + z_lo), core: 2. Of those that a mesh axis runs over, the one named last changes fastest.
Arguments:
- row_features: bfloat16 [512, 256], P(('row', 'col')), may hold values from -6 to 6
- col_features: bfloat16 [2048, 256], P(('col', 'row')), may hold values from -6 to 6
- row_proj: bfloat16 [256, 64], replicated, may hold values from -0.375 to 0.375
- col_proj: bfloat16 [256, 64], replicated, may hold values from -0.375 to 0.375
- pair_weight: bfloat16 [2, 3, 3, 64, 64], replicated, may hold values from -0.1875 to 0.1875
- pair_bias: float32 [64], replicated, may hold values from -4 to 4
- conv_weight: bfloat16 [3, 3, 64, 64], replicated, may hold values from -0.25 to 0.25
- dilations: int32 [2], replicated, may hold values from 1 to 8, as said below
- cotangent: bfloat16 [64, 512, 2048], P(None, 'row', 'col'), may hold values from -6 to 6
Outputs:
- pair_out: bfloat16 [64, 512, 2048], P(None, 'row', 'col')
- grad_row_features: float32 [512, 256], P(('row', 'col'))
- grad_col_features: float32 [2048, 256], P(('col', 'row'))
- grad_row_proj: float32 [256, 64], replicated
- grad_col_proj: float32 [256, 64], replicated
- grad_pair_weight: float32 [2, 3, 3, 64, 64], replicated
- grad_pair_bias: float32 [64], replicated
- grad_conv_weight: float32 [3, 3, 64, 64], replicated
Inputs may be any that keep to these rules, and one draw needn't show every extreme that they name: One of the two dilations equals 8.
All inputs are finite; a program needn't handle non-finite values.
Results may differ from a plain program's by a relative error of at most 0.0054.
Values may be sent and summed in bfloat16 or wider, within the bound.
A program may use at most 64 MiB of HBM per device.

v0:
```python
import jax
import jax.numpy as jnp
from jax import lax
from jax.sharding import PartitionSpec as P

MAX_DILATION = 8


def sent_to_all(value, axis):
    copies = jnp.broadcast_to(value, (lax.axis_size(axis), *value.shape))
    return lax.all_to_all(copies, axis, split_axis=0, concat_axis=0, tiled=True)


def in_order(tiles, dim):
    dims = list(tiles.shape[1:])
    dims[dim] *= tiles.shape[0]
    return jnp.moveaxis(tiles, 0, dim).reshape(dims)


def gathered_copies(value, axis, dim):
    tiles = sent_to_all(value, axis)
    return in_order(tiles, dim)


def padded_2(value, sides, width):
    for axis, dim in sides:
        devices, length = (lax.axis_size(axis), value.shape[dim])
        up = [(i, (i + 1) % devices) for i in range(devices - 1)]
        down = [(j, i) for i, j in up]
        last = lax.slice_in_dim(value, length - width, length, axis=dim)
        leading = lax.slice_in_dim(value, 0, width, axis=dim)
        before = lax.ppermute(last, axis, up)
        after = lax.ppermute(leading, axis, down)
        value = jnp.concatenate([before, value, after], axis=dim)
    return value


def over_copies(value, axis):
    everything = sent_to_all(value, axis)
    return jnp.sum(everything, axis=0)


def total_of_pieces(value, axis):
    tiles = lax.all_gather(value, axis)
    return tiles.sum(axis=0)


def project(features, weight):
    return jnp.dot(features, weight, preferred_element_type=jnp.float32).astype(jnp.bfloat16)


def line_terms(padded, weights, dilation, count, offset):
    shifted = jnp.stack(
        [
            lax.dynamic_slice_in_dim(padded, offset + (tap_idx - 1) * dilation, count, 0)
            for tap_idx in range(3)
        ]
    )
    return jnp.einsum("kip,kqpo->qio", shifted, weights, preferred_element_type=jnp.float32)


def line_valid(first_cell, count, cell_limit, dilation):
    cells = first_cell + jnp.arange(count, dtype=jnp.int32)
    columns = [
        (cells + (tap_idx - 1) * dilation >= 0) & (cells + (tap_idx - 1) * dilation < cell_limit)
        for tap_idx in range(3)
    ]
    return jnp.stack(columns, axis=1).astype(jnp.float32)


def inside_mask(first_cell, count, cell_limit):
    cells = first_cell + jnp.arange(count, dtype=jnp.int32)
    return ((cells >= 0) & (cells < cell_limit)).astype(jnp.float32)


def pair_field(row_terms, col_terms, row_valid, col_valid, bias):
    from_rows = jnp.einsum("jq,qic->cij", col_valid, row_terms, precision=lax.Precision.HIGHEST)
    from_cols = jnp.einsum("ik,kjc->cij", row_valid, col_terms, precision=lax.Precision.HIGHEST)
    return from_rows + from_cols + bias[:, None, None]


def window_at(padded, row_index, col_index, rows, cols):
    anchor = jnp.zeros((), jnp.int32)
    return lax.dynamic_slice(padded, (anchor, row_index, col_index), (padded.shape[0], rows, cols))


def conv_taps(padded, weight, dilation, rows, cols, margin):
    result = jnp.zeros((weight.shape[3], rows, cols), jnp.float32)
    for tap_row in range(3):
        for tap_col in range(3):
            window = window_at(
                padded,
                margin + (tap_row - 1) * dilation,
                margin + (tap_col - 1) * dilation,
                rows,
                cols,
            )
            result = result + jnp.einsum(
                "co,cij->oij", weight[tap_row, tap_col], window, preferred_element_type=jnp.float32
            )
    return result


def back_taps(padded, weight, dilation, rows, cols, margin):
    result = jnp.zeros((weight.shape[2], rows, cols), jnp.float32)
    for tap_row in range(3):
        for tap_col in range(3):
            window = window_at(
                padded,
                margin - (tap_row - 1) * dilation,
                margin - (tap_col - 1) * dilation,
                rows,
                cols,
            )
            result = result + jnp.einsum(
                "co,oij->cij", weight[tap_row, tap_col], window, preferred_element_type=jnp.float32
            )
    return result


def tap_grads(hidden_pad, grads, dilation, rows, cols, margin):
    stacked = []
    for tap_row in range(3):
        line_list = []
        for tap_col in range(3):
            window = window_at(
                hidden_pad,
                margin + (tap_row - 1) * dilation,
                margin + (tap_col - 1) * dilation,
                rows,
                cols,
            )
            line_list.append(
                jnp.einsum("cij,oij->co", window, grads, preferred_element_type=jnp.float32)
            )
        stacked.append(jnp.stack(line_list))
    return jnp.stack(stacked)


def shards(
    row_features,
    col_features,
    row_proj,
    col_proj,
    pair_weight,
    pair_bias,
    conv_weight,
    dilations,
    cotangent,
):
    first_rate = dilations[0]
    second_rate = dilations[1]
    margin = MAX_DILATION
    row_count = lax.axis_size("row")
    col_count = lax.axis_size("col")
    row_place = lax.axis_index("row")
    col_place = lax.axis_index("col")
    rows_here = cotangent.shape[1]
    cols_here = cotangent.shape[2]
    row_start = row_place * rows_here
    col_start = col_place * cols_here
    row_limit = rows_here * row_count
    col_limit = cols_here * col_count
    row_piece = row_features.shape[0]
    col_piece = col_features.shape[0]
    rows_a = gathered_copies(project(row_features, row_proj), "col", 0)
    cols_b = gathered_copies(project(col_features, col_proj), "row", 0)
    pad_reach = 2 * margin
    a_pad = padded_2(rows_a, (("row", 0),), 2 * MAX_DILATION)
    b_pad = padded_2(cols_b, (("col", 0),), 2 * MAX_DILATION)
    row_terms = line_terms(
        a_pad, pair_weight[0], first_rate, rows_here + 2 * margin, pad_reach - margin
    )
    col_terms = line_terms(
        b_pad,
        jnp.swapaxes(pair_weight[1], 0, 1),
        first_rate,
        cols_here + 2 * margin,
        pad_reach - margin,
    )
    row_valid = line_valid(row_start - margin, rows_here + 2 * margin, row_limit, first_rate)
    col_valid = line_valid(col_start - margin, cols_here + 2 * margin, col_limit, first_rate)
    pre_act = pair_field(row_terms, col_terms, row_valid, col_valid, pair_bias)
    row_inside = inside_mask(row_start - margin, rows_here + 2 * margin, row_limit)
    col_inside = inside_mask(col_start - margin, cols_here + 2 * margin, col_limit)
    hidden = (jax.nn.silu(pre_act) * row_inside[None, :, None] * col_inside[None, None, :]).astype(
        jnp.bfloat16
    )
    pre_own = pre_act[:, margin : margin + rows_here, margin : margin + cols_here]
    hidden_own = hidden[:, margin : margin + rows_here, margin : margin + cols_here]
    conv_mixed = conv_taps(hidden, conv_weight, second_rate, rows_here, cols_here, margin)
    pair_out = (hidden_own.astype(jnp.float32) + conv_mixed).astype(jnp.bfloat16)
    grad_pad = padded_2(cotangent, (("row", 1), ("col", 2)), MAX_DILATION)
    d_hidden = cotangent.astype(jnp.float32) + back_taps(
        grad_pad, conv_weight, second_rate, rows_here, cols_here, margin
    )
    conv_grad = tap_grads(hidden, cotangent, second_rate, rows_here, cols_here, margin)
    sigmoid_own = jax.nn.sigmoid(pre_own)
    d_pre = d_hidden * sigmoid_own * (1.0 + pre_own * (1.0 - sigmoid_own))
    bias_grad = jnp.sum(d_pre, axis=(1, 2))
    row_valid_own = line_valid(row_start, rows_here, row_limit, first_rate)
    col_valid_own = line_valid(col_start, cols_here, col_limit, first_rate)
    row_part = jnp.einsum("jq,cij->qic", col_valid_own, d_pre, precision=lax.Precision.HIGHEST)
    col_part = jnp.einsum("ik,cij->kjc", row_valid_own, d_pre, precision=lax.Precision.HIGHEST)
    row_sums = over_copies(row_part, "col")
    col_sums = total_of_pieces(col_part, "row")
    back_rows = jnp.einsum(
        "qio,kqpo->kip",
        row_sums,
        pair_weight[0].astype(jnp.float32),
        precision=lax.Precision.HIGHEST,
    )
    back_cols = jnp.einsum(
        "kjo,kqpo->qjp",
        col_sums,
        pair_weight[1].astype(jnp.float32),
        precision=lax.Precision.HIGHEST,
    )
    rows_back_pad = padded_2(back_rows, (("row", 1),), MAX_DILATION)
    cols_back_pad = padded_2(back_cols, (("col", 1),), MAX_DILATION)
    row_own = col_place * row_piece
    col_own = row_place * col_piece
    d_rows = sum(
        (
            lax.dynamic_slice_in_dim(
                rows_back_pad[tap_idx], margin + row_own - (tap_idx - 1) * first_rate, row_piece, 0
            )
            for tap_idx in range(3)
        )
    )
    d_cols = sum(
        (
            lax.dynamic_slice_in_dim(
                cols_back_pad[tap_idx], margin + col_own - (tap_idx - 1) * first_rate, col_piece, 0
            )
            for tap_idx in range(3)
        )
    )
    d_rows = d_rows.astype(jnp.bfloat16)
    d_cols = d_cols.astype(jnp.bfloat16)
    grad_row_features = jnp.dot(d_rows, row_proj.T, preferred_element_type=jnp.float32)
    grad_col_features = jnp.dot(d_cols, col_proj.T, preferred_element_type=jnp.float32)
    grad_row_proj = jnp.dot(row_features.T, d_rows, preferred_element_type=jnp.float32)
    grad_col_proj = jnp.dot(col_features.T, d_cols, preferred_element_type=jnp.float32)
    row_shifted = jnp.stack(
        [
            lax.dynamic_slice_in_dim(
                a_pad, pad_reach + row_own + (tap_idx - 1) * first_rate, row_piece, 0
            )
            for tap_idx in range(3)
        ]
    )
    col_shifted = jnp.stack(
        [
            lax.dynamic_slice_in_dim(
                b_pad, pad_reach + col_own + (tap_idx - 1) * first_rate, col_piece, 0
            )
            for tap_idx in range(3)
        ]
    )
    row_sums_own = lax.dynamic_slice_in_dim(row_sums, row_own, row_piece, 1)
    col_sums_own = lax.dynamic_slice_in_dim(col_sums, col_own, col_piece, 1)
    grad_row_pair = jnp.einsum(
        "kip,qio->kqpo",
        row_shifted.astype(jnp.float32),
        row_sums_own,
        precision=lax.Precision.HIGHEST,
    )
    grad_col_pair = jnp.einsum(
        "qjp,kjo->kqpo",
        col_shifted.astype(jnp.float32),
        col_sums_own,
        precision=lax.Precision.HIGHEST,
    )
    summed = lax.psum(
        (
            grad_row_proj,
            grad_col_proj,
            jnp.stack([grad_row_pair, grad_col_pair]),
            bias_grad,
            conv_grad,
        ),
        ("row", "col"),
    )
    return (
        pair_out,
        grad_row_features,
        grad_col_features,
        summed[0],
        summed[1],
        summed[2],
        summed[3],
        summed[4],
    )


def solution(mesh):
    return jax.shard_map(
        shards,
        mesh=mesh,
        in_specs=(
            P(("row", "col"), None),
            P(("col", "row"), None),
            P(),
            P(),
            P(),
            P(),
            P(),
            P(),
            P(None, "row", "col"),
        ),
        out_specs=(
            P(None, "row", "col"),
            P(("row", "col"), None),
            P(("col", "row"), None),
            P(),
            P(),
            P(),
            P(),
            P(),
        ),
        check_vma=False,
    )
```

profile of v0, /device:TPU:1, one launch (start us, length us, event | category | flops | bytes accessed | tf_op | source)
XLA Modules:
  0.0 496.6 jit_solution(1693750690878822578)
XLA Ops:
  8.8 6.4 %all-to-all-start = ((bf16[8,2,64]{2,1,0:T(2,128)(2,1)}), bf16[8,2,64]{2,1,0:T(2,128)(2,1)S(1)}, u32[]{:S(2)}, u32[]{:S(2)}) async-start(bf16[8,2,64]{2,1,0:T(2,128)(2,1)} %broadcast_in_dim.12), calls=%async_computation | async-start | bytes 8192 | tf_op jit(solution)/shard_map/all_to_all | solution.py:11
  16.3 4.0 collective-permute-start.4
  20.3 1.9 collective-permute-start.5
  29.1 12.6 %all-to-all-start.1 = ((bf16[32,2,256]{2,1,0:T(2,128)(2,1)}), bf16[32,2,256]{2,1,0:T(2,128)(2,1)S(1)}, u32[]{:S(2)}, u32[]{:S(2)}) async-start(bf16[32,2,256]{2,1,0:T(2,128)(2,1)} %reshape.293), calls=%async_computation.1 | async-start | bytes 65536 | tf_op jit(solution)/shard_map/all_to_all | solution.py:11
  41.8 3.5 collective-permute-start
  45.3 1.9 collective-permute-start.1
  52.3 3.6 collective-permute-start.2
  58.2 2.3 collective-permute-done.3
  61.0 1.5 fusion.46
  63.0 4.0 collective-permute-start.6
  68.6 4.6 multiply_convert_fusion
  73.2 3.8 collective-permute-done.6
  77.0 12.3 %collective-permute-done.7 = bf16[64,32,8]{2,0,1:T(8,128)(2,1)S(1)} collective-permute-done((bf16[64,32,8]{2,0,1:T(8,128)(2,1)S(1)}, bf16[64,32,8]{2,0,1:T(8,128)(2,1)S(1)}, u32[]{:S(2)}, u32[]{:S(2)}) %collective-permute-start.7) | collective-permute-done | bytes 32800 | tf_op jit(solution)/shard_map/ppermute | solution.py:33
  93.2 1.8 fusion.208
  114.7 4.1 all-to-all-start.2
  119.6 4.9 all-to-all-done.2
  126.4 6.4 %collective-permute-start.8 = (f32[3,8,64]{2,1,0:T(8,128)S(1)}, f32[3,8,64]{2,1,0:T(8,128)S(1)}, u32[]{:S(2)}, u32[]{:S(2)}) collective-permute-start(f32[3,8,64]{2,1,0:T(8,128)S(1)} %get-tuple-element.74), channel_id=1, source_target_pairs={{0,8},{8,16},{16,24},{24,32},{32,40},{40,48},{48,56},{56,64},{64,7... | collective-permute-start | bytes 18440 | tf_op jit(solution)/shard_map/ppermute | solution.py:32
  132.8 1.9 collective-permute-start.9
  136.1 78.0 %psum.38 = f32[64]{0:T(128)} all-reduce(f32[64]{0:T(128)S(1)} %copy-done.22), channel_id=1, replica_groups=mesh['row'=32,'col'=8] {'row','col'}, use_global_device_ids=true, to_apply=%region_6.7 | all-reduce | flops 64 | bytes 512 | tf_op jit(solution)/shard_map/psum | solution.py:275
  215.4 3.2 reduce_sum.28
  219.0 2.7 collective-permute-start.10
  224.3 2.8 collective-permute-done.11
  229.7 254.2 %all-reduce.3.cloned.1.call-done = (f32[256,64]{0,1:T(8,128)}, f32[256,64]{0,1:T(8,128)}, f32[2,3,3,64,64]{3,4,1,2,0:T(8,128)}, f32[3,3,64,64]{3,2,1,0:T(8,128)}) async-done(((f32[256,64]{0,1:T(8,128)}, f32[256,64]{0,1:T(8,128)}, f32[2,3,3,64,64]{3,4,1,2,0:T(8,128)}, f32[3,3,64,64]{3,2,1,0:T(8,128)}), (f32[256,64]{0,1:T(8,128)}, f32[256,64]{0,1:T(8,128)}, f32[2,3,3,64,64]{3,4,1,2,0:T(8,128)}, ...) | async-done | bytes 573456 | tf_op jit(solution)/shard_map/psum | solution.py:275
  483.9 2.1 copy.247
  (168 shorter events, 47.2 us)
Async XLA Ops:
  7.2 20.5 %copy-start = (bf16[256,64]{0,1:T(8,128)(2,1)S(1)}, bf16[256,64]{0,1:T(8,128)(2,1)}, u32[]{:S(2)}) copy-start(bf16[256,64]{0,1:T(8,128)(2,1)} %param.12) | copy-start | bytes 98308
  7.2 19.5 %copy-start.1 = (bf16[64,16,256]{2,1,0:T(8,128)(2,1)S(1)}, bf16[64,16,256]{2,1,0:T(8,128)(2,1)}, u32[]{:S(2)}) copy-start(bf16[64,16,256]{2,1,0:T(8,128)(2,1)} %param.17) | copy-start | bytes 1572868
  8.8 20.3 %all-to-all-start = ((bf16[8,2,64]{2,1,0:T(2,128)(2,1)}), bf16[8,2,64]{2,1,0:T(2,128)(2,1)S(1)}, u32[]{:S(2)}, u32[]{:S(2)}) async-start(bf16[8,2,64]{2,1,0:T(2,128)(2,1)} %broadcast_in_dim.12), calls=%async_computation | async-start | bytes 8192 | tf_op jit(solution)/shard_map/all_to_all | solution.py:11
  16.3 46.2 %collective-permute-start.4 = (bf16[64,8,256]{2,0,1:T(8,128)(2,1)S(1)}, bf16[64,8,256]{2,0,1:T(8,128)(2,1)S(1)}, u32[]{:S(2)}, u32[]{:S(2)}) collective-permute-start(bf16[64,8,256]{2,0,1:T(8,128)(2,1)S(1)} %copy.319), channel_id=1, source_target_pairs={{0,8},{8,16},{16,24},{24,32},{32,40},{40,48},{48,56},{56,64},{64,7... | collective-permute-start | bytes 786440 | tf_op jit(solution)/shard_map/ppermute | solution.py:32
  20.3 42.4 %collective-permute-start.5 = (bf16[64,8,256]{2,0,1:T(8,128)(2,1)S(1)}, bf16[64,8,256]{2,0,1:T(8,128)(2,1)S(1)}, u32[]{:S(2)}, u32[]{:S(2)}) collective-permute-start(bf16[64,8,256]{2,0,1:T(8,128)(2,1)S(1)} %copy.320), channel_id=1, source_target_pairs={{8,0},{16,8},{24,16},{32,24},{40,32},{48,40},{56,48},{64,56},{72,6... | collective-permute-start | bytes 786440 | tf_op jit(solution)/shard_map/ppermute | solution.py:33
  29.1 22.9 %all-to-all-start.1 = ((bf16[32,2,256]{2,1,0:T(2,128)(2,1)}), bf16[32,2,256]{2,1,0:T(2,128)(2,1)S(1)}, u32[]{:S(2)}, u32[]{:S(2)}) async-start(bf16[32,2,256]{2,1,0:T(2,128)(2,1)} %reshape.293), calls=%async_computation.1 | async-start | bytes 65536 | tf_op jit(solution)/shard_map/all_to_all | solution.py:11
  41.7 173.7 %all-gather.3.cloned.1.call-start = ((), (), s32[]{:S(2)}) async-start(), calls=%async_computation.3 | async-start | bytes 6488064 | tf_op jit(solution)/shard_map/all_gather | solution.py:44
  41.8 10.2 %collective-permute-start = (bf16[16,64]{1,0:T(8,128)(2,1)S(1)}, bf16[16,64]{1,0:T(8,128)(2,1)S(1)}, u32[]{:S(2)}, u32[]{:S(2)}) collective-permute-start(bf16[16,64]{1,0:T(8,128)(2,1)S(1)} %bitcast.322), channel_id=1, source_target_pairs={{0,8},{8,16},{16,24},{24,32},{32,40},{40,48},{48,56},{56,64},{64,7... | collective-permute-start | bytes 6152 | tf_op jit(solution)/shard_map/ppermute | solution.py:32
  45.3 6.7 %collective-permute-start.1 = (bf16[16,64]{1,0:T(8,128)(2,1)S(1)}, bf16[16,64]{1,0:T(8,128)(2,1)S(1)}, u32[]{:S(2)}, u32[]{:S(2)}) collective-permute-start(bf16[16,64]{1,0:T(8,128)(2,1)S(1)} %bitcast.323), channel_id=1, source_target_pairs={{8,0},{16,8},{24,16},{32,24},{40,32},{48,40},{56,48},{64,56},{72,6... | collective-permute-start | bytes 6152 | tf_op jit(solution)/shard_map/ppermute | solution.py:33
  52.3 6.0 %collective-permute-start.2 = (bf16[16,64]{0,1:T(8,128)(2,1)S(1)}, bf16[16,64]{0,1:T(8,128)(2,1)S(1)}, u32[]{:S(2)}, u32[]{:S(2)}) collective-permute-start(bf16[16,64]{0,1:T(8,128)(2,1)S(1)} %copy.199), channel_id=1, source_target_pairs={{0,1},{1,2},{2,3},{3,4},{4,5},{5,6},{6,7},{8,9},{9,10},{10,11},{11... | collective-permute-start | bytes 6152 | tf_op jit(solution)/shard_map/ppermute | solution.py:32
  56.0 4.5 collective-permute-start.3
  63.0 14.0 %collective-permute-start.6 = (bf16[64,32,8]{2,0,1:T(8,128)(2,1)S(1)}, bf16[64,32,8]{2,0,1:T(8,128)(2,1)S(1)}, u32[]{:S(2)}, u32[]{:S(2)}) collective-permute-start(bf16[64,32,8]{2,0,1:T(8,128)(2,1)S(1)} %get-tuple-element.52), channel_id=1, source_target_pairs={{0,1},{1,2},{2,3},{3,4},{4,5},{5,6},{6,7},{8,9},{9,10},{10,11},{11... | collective-permute-start | bytes 98312 | tf_op jit(solution)/shard_map/ppermute | solution.py:32
  67.0 22.3 %collective-permute-start.7 = (bf16[64,32,8]{2,0,1:T(8,128)(2,1)S(1)}, bf16[64,32,8]{2,0,1:T(8,128)(2,1)S(1)}, u32[]{:S(2)}, u32[]{:S(2)}) collective-permute-start(bf16[64,32,8]{2,0,1:T(8,128)(2,1)S(1)} %get-tuple-element.53), channel_id=1, source_target_pairs={{1,0},{2,1},{3,2},{4,3},{5,4},{6,5},{7,6},{9,8},{10,9},{11,10},{12... | collective-permute-start | bytes 98312 | tf_op jit(solution)/shard_map/ppermute | solution.py:33
  114.7 21.4 %copy-start.22 = (f32[64]{0:T(128)S(1)}, f32[64]{0:T(128)}, u32[]{:S(2)}) copy-start(f32[64]{0:T(128)} %get-tuple-element.86) | copy-start | bytes 772
  114.7 99.4 %copy-start.13 = (bf16[1,2,64]{2,1,0:T(2,128)(2,1)S(1)}, bf16[1,2,64]{2,1,0:T(2,128)(2,1)}, u32[]{:S(2)}) copy-start(bf16[1,2,64]{2,1,0:T(2,128)(2,1)} %get-tuple-element.76) | copy-start | bytes 772
  114.7 99.4 %copy-start.14 = (bf16[1,2,64]{2,1,0:T(2,128)(2,1)S(1)}, bf16[1,2,64]{2,1,0:T(2,128)(2,1)}, u32[]{:S(2)}) copy-start(bf16[1,2,64]{2,1,0:T(2,128)(2,1)} %get-tuple-element.77) | copy-start | bytes 772
  114.7 99.4 %copy-start.15 = (bf16[1,2,64]{2,1,0:T(2,128)(2,1)S(1)}, bf16[1,2,64]{2,1,0:T(2,128)(2,1)}, u32[]{:S(2)}) copy-start(bf16[1,2,64]{2,1,0:T(2,128)(2,1)} %get-tuple-element.78) | copy-start | bytes 772
  114.7 9.8 %all-to-all-start.2 = ((f32[8,1,3072]{2,1,0:T(1,128)}), f32[8,1,3072]{2,1,0:T(1,128)S(1)}, u32[]{:S(2)}, u32[]{:S(2)}) async-start(f32[8,1,3072]{2,1,0:T(1,128)} %reshape.295), calls=%async_computation.2 | async-start | bytes 196608 | tf_op jit(solution)/shard_map/all_to_all | solution.py:11
  118.8 365.2 %all-reduce.3.cloned.1.call-start = ((), (), s32[]{:S(2)}) async-start(), calls=%async_computation.4 | async-start | bytes 2031616 | tf_op jit(solution)/shard_map/psum | solution.py:275
  118.9 95.7 %copy-start.18 = (bf16[2,256]{1,0:T(2,128)(2,1)S(1)}, bf16[2,256]{1,0:T(2,128)(2,1)}, u32[]{:S(2)}) copy-start(bf16[2,256]{1,0:T(2,128)(2,1)} %param.9) | copy-start | bytes 3076
  126.4 88.1 %collective-permute-start.8 = (f32[3,8,64]{2,1,0:T(8,128)S(1)}, f32[3,8,64]{2,1,0:T(8,128)S(1)}, u32[]{:S(2)}, u32[]{:S(2)}) collective-permute-start(f32[3,8,64]{2,1,0:T(8,128)S(1)} %get-tuple-element.74), channel_id=1, source_target_pairs={{0,8},{8,16},{16,24},{24,32},{32,40},{40,48},{48,56},{56,64},{64,7... | collective-permute-start | bytes 18440 | tf_op jit(solution)/shard_map/ppermute | solution.py:32
  132.8 81.7 %collective-permute-start.9 = (f32[3,8,64]{2,1,0:T(8,128)S(1)}, f32[3,8,64]{2,1,0:T(8,128)S(1)}, u32[]{:S(2)}, u32[]{:S(2)}) collective-permute-start(f32[3,8,64]{2,1,0:T(8,128)S(1)} %get-tuple-element.75), channel_id=1, source_target_pairs={{8,0},{16,8},{24,16},{32,24},{40,32},{48,40},{56,48},{64,56},{72,6... | collective-permute-start | bytes 18440 | tf_op jit(solution)/shard_map/ppermute | solution.py:33
  219.0 5.3 %collective-permute-start.10 = (f32[3,8,64]{1,2,0:T(8,128)S(1)}, f32[3,8,64]{1,2,0:T(8,128)S(1)}, u32[]{:S(2)}, u32[]{:S(2)}) collective-permute-start(f32[3,8,64]{1,2,0:T(8,128)S(1)} %get-tuple-element.61), channel_id=1, source_target_pairs={{0,1},{1,2},{2,3},{3,4},{4,5},{5,6},{6,7},{8,9},{9,10},{10,11},{11... | collective-permute-start | bytes 18440 | tf_op jit(solution)/shard_map/ppermute | solution.py:32
  221.7 5.4 %collective-permute-start.11 = (f32[3,8,64]{1,2,0:T(8,128)S(1)}, f32[3,8,64]{1,2,0:T(8,128)S(1)}, u32[]{:S(2)}, u32[]{:S(2)}) collective-permute-start(f32[3,8,64]{1,2,0:T(8,128)S(1)} %get-tuple-element.62), channel_id=1, source_target_pairs={{1,0},{2,1},{3,2},{4,3},{5,4},{6,5},{7,6},{9,8},{10,9},{11,10},{12... | collective-permute-start | bytes 18440 | tf_op jit(solution)/shard_map/ppermute | solution.py:33
  (17 other events, 132.3 us)
Sparse Core Ops, SparseCore 0:
  96.9 71.5 all-gather.2
  228.3 255.5 all-reduce.2
where the time goes:
time: 498 us; the launch traced here: 497 us
  waiting for transfers between devices  280 us (56%)
  blocking collectives  78 us (16%)
  starting transfers between devices  57.2 us (11%)
  matrix products  29 us (6%)
  between operations  24.8 us (5%)
  local copies, waits for them, and re-layouts  14.5 us (3%)
  other arithmetic  12.7 us (3%)
    psum x1, waiting for transfers between devices, shards(): lax.psum((grad_row_proj, grad_col_proj, jnp.stack([grad_row_pair, grad_co...  254 us
    psum x1, blocking collectives, shards(): lax.psum((grad_row_proj, grad_col_proj, jnp.stack([grad_row_pair, grad_co...  78 us
    ppermute x6, starting transfers between devices, padded_2(): before = lax.ppermute(last, axis, up)  24.3 us
    all_to_all x3, starting transfers between devices, sent_to_all(): return lax.all_to_all(copies, axis, split_axis=0, concat_axis=0, tiled=True)  23 us
    ppermute x6, waiting for transfers between devices, padded_2(): after = lax.ppermute(leading, axis, down)  17.4 us
  transfers between devices with their start and end apart: 17, of which 6 were waited for; matrix products, arithmetic and copies ran while one was open for 7% of the time, Pallas kernels for 0%

commit v1 on v0

--- a/solution.py
+++ b/solution.py
@@ -1,48 +1,276 @@
+import functools
+
 import jax
 import jax.numpy as jnp
 from jax import lax
+from jax.experimental import pallas as pl
+from jax.experimental.pallas import tpu as pltpu
 from jax.sharding import PartitionSpec as P
 
 MAX_DILATION = 8
-
-
-def sent_to_all(value, axis):
-    copies = jnp.broadcast_to(value, (lax.axis_size(axis), *value.shape))
-    return lax.all_to_all(copies, axis, split_axis=0, concat_axis=0, tiled=True)
-
-
-def in_order(tiles, dim):
-    dims = list(tiles.shape[1:])
-    dims[dim] *= tiles.shape[0]
-    return jnp.moveaxis(tiles, 0, dim).reshape(dims)
-
-
-def gathered_copies(value, axis, dim):
-    tiles = sent_to_all(value, axis)
-    return in_order(tiles, dim)
-
-
-def padded_2(value, sides, width):
-    for axis, dim in sides:
-        devices, length = (lax.axis_size(axis), value.shape[dim])
-        up = [(i, (i + 1) % devices) for i in range(devices - 1)]
-        down = [(j, i) for i, j in up]
-        last = lax.slice_in_dim(value, length - width, length, axis=dim)
-        leading = lax.slice_in_dim(value, 0, width, axis=dim)
-        before = lax.ppermute(last, axis, up)
-        after = lax.ppermute(leading, axis, down)
-        value = jnp.concatenate([before, value, after], axis=dim)
-    return value
-
-
-def over_copies(value, axis):
-    everything = sent_to_all(value, axis)
-    return jnp.sum(everything, axis=0)
-
-
-def total_of_pieces(value, axis):
-    tiles = lax.all_gather(value, axis)
-    return tiles.sum(axis=0)
+MESH = pl.DeviceIdType.MESH
+VMEM = pltpu.VMEM
+
+
+def places():
+    r = lax.axis_index("row")
+    c = lax.axis_index("col")
+    return r, c, r // 8, lax.rem(r // 2, 4), lax.rem(r, 2), c // 2, lax.rem(c, 2)
+
+
+def device_at(z_hi, x, core, y, z_lo):
+    return ((z_hi * 4 + x) * 2 + core, y * 2 + z_lo)
+
+
+def signal(barrier, target):
+    pl.semaphore_signal(barrier, inc=1, device_id=target, device_id_type=MESH)
+
+
+def push(src, dst, send_sem, recv_sem, target):
+    pltpu.make_async_remote_copy(
+        src_ref=src,
+        dst_ref=dst,
+        send_sem=send_sem,
+        recv_sem=recv_sem,
+        device_id=target,
+        device_id_type=MESH,
+    ).start()
+
+
+def await_bytes(ref, sem):
+    pltpu.make_async_copy(ref, ref, sem).wait()
+
+
+def gather_kernel(rf_ref, cf_ref, cot_ref, rows_ref, cols_ref, halo_ref, side_ref, pack, ssem, rsem):
+    r, c, _, _, _, _, _ = places()
+    up, down = lax.rem(r + 31, 32), lax.rem(r + 1, 32)
+    left, right = lax.rem(c + 7, 8), lax.rem(c + 1, 8)
+    barrier = pltpu.get_barrier_semaphore()
+
+    @pl.loop(1, 32)
+    def _(t):
+        signal(barrier, (lax.rem(r + t, 32), c))
+
+    @pl.loop(1, 8)
+    def _(t):
+        signal(barrier, (r, lax.rem(c + t, 8)))
+
+    for r_to in (up, down):
+        for c_to in (left, right):
+            signal(barrier, (r_to, c_to))
+
+    lane = lax.broadcasted_iota(jnp.int32, (64, 128), 1) // 8
+    first = jnp.zeros((64, 128), jnp.float32)
+    last = jnp.zeros((64, 128), jnp.float32)
+    for i in range(16):
+        head = cot_ref[i, :, 0:128].astype(jnp.float32)
+        tail = cot_ref[i, :, 128:256].astype(jnp.float32)
+        first = jnp.where(lane == i, pltpu.roll(head, 8 * i, 1) if i else head, first)
+        last = jnp.where(lane == i, pltpu.roll(tail, (8 * i + 8) % 128, 1) if i < 15 else tail, last)
+    pack[0] = first.astype(jnp.bfloat16)
+    pack[1] = last.astype(jnp.bfloat16)
+    rows_ref[1, c] = rf_ref[...]
+    cols_ref[r + 2] = cf_ref[...]
+    pl.semaphore_wait(barrier, 31 + 7 + 4)
+
+    push(cot_ref.at[pl.ds(8, 8)], halo_ref.at[0], ssem.at[0], rsem.at[0], (down, c))
+    push(cot_ref.at[pl.ds(0, 8)], halo_ref.at[1], ssem.at[1], rsem.at[1], (up, c))
+
+    @pl.loop(1, 32)
+    def _(t):
+        push(cf_ref, cols_ref.at[r + 2], ssem.at[2], rsem.at[2], (lax.rem(r + t, 32), c))
+
+    @pl.loop(1, 8)
+    def _(t):
+        push(rf_ref, rows_ref.at[1, c], ssem.at[3], rsem.at[3], (r, lax.rem(c + t, 8)))
+
+    for slot, r_to in ((2, up), (1, r), (0, down)):
+        push(pack.at[0], side_ref.at[1, slot], ssem.at[4], rsem.at[4], (r_to, left))
+        push(pack.at[1], side_ref.at[0, slot], ssem.at[4], rsem.at[4], (r_to, right))
+
+    await_bytes(rows_ref.at[1, pl.ds(0, 7)], rsem.at[3])
+    push(rows_ref.at[1], rows_ref.at[0], ssem.at[5], rsem.at[5], (down, c))
+    push(rows_ref.at[1], rows_ref.at[2], ssem.at[6], rsem.at[6], (up, c))
+    await_bytes(cols_ref.at[pl.ds(2, 31)], rsem.at[2])
+    push(cols_ref.at[pl.ds(2, 2)], cols_ref.at[pl.ds(34, 2)], ssem.at[7], rsem.at[7], (r, left))
+    push(cols_ref.at[pl.ds(32, 2)], cols_ref.at[pl.ds(0, 2)], ssem.at[8], rsem.at[8], (r, right))
+
+    await_bytes(halo_ref.at[0], rsem.at[0])
+    await_bytes(halo_ref.at[1], rsem.at[1])
+    await_bytes(side_ref, rsem.at[4])
+    await_bytes(rows_ref.at[0], rsem.at[5])
+    await_bytes(rows_ref.at[2], rsem.at[6])
+    await_bytes(cols_ref.at[pl.ds(34, 2)], rsem.at[7])
+    await_bytes(cols_ref.at[pl.ds(0, 2)], rsem.at[8])
+    await_bytes(halo_ref.at[0], ssem.at[0])
+    await_bytes(halo_ref.at[1], ssem.at[1])
+    await_bytes(cols_ref.at[pl.ds(2, 31)], ssem.at[2])
+    await_bytes(rows_ref.at[1, pl.ds(0, 7)], ssem.at[3])
+    await_bytes(side_ref, ssem.at[4])
+    await_bytes(rows_ref.at[0], ssem.at[5])
+    await_bytes(rows_ref.at[2], ssem.at[6])
+    await_bytes(cols_ref.at[pl.ds(34, 2)], ssem.at[7])
+    await_bytes(cols_ref.at[pl.ds(0, 2)], ssem.at[8])
+
+
+def gather_all(rf, cf, cot):
+    vm = pl.BlockSpec(memory_space=VMEM)
+    return pl.pallas_call(
+        gather_kernel,
+        out_shape=(
+            jax.ShapeDtypeStruct((3, 8, 2, 256), jnp.float32),
+            jax.ShapeDtypeStruct((36, 16, 128), jnp.bfloat16),
+            jax.ShapeDtypeStruct((2, 8, 64, 256), jnp.bfloat16),
+            jax.ShapeDtypeStruct((2, 3, 64, 128), jnp.bfloat16),
+        ),
+        in_specs=[vm] * 3,
+        out_specs=(vm,) * 4,
+        scratch_shapes=[
+            VMEM((2, 64, 128), jnp.bfloat16),
+            pltpu.SemaphoreType.DMA((9,)),
+            pltpu.SemaphoreType.DMA((9,)),
+        ],
+        compiler_params=pltpu.CompilerParams(
+            collective_id=1, has_side_effects=True, vmem_limit_bytes=40 << 20
+        ),
+        name="gather_all",
+    )(rf, cf, cot)
+
+
+def reduce_kernel(
+    g_ref, c_ref, r_ref, out_ref, drow_ref, dcol_ref,
+    g0, g1, gz, c0, c1, c2, r1, r2, red, halo, ssem, rsem,
+):
+    r, c, z_hi, x, core, y, z_lo = places()
+    a = x * 4 + y
+    z = z_hi * 2 + z_lo
+    sibling = device_at(z_hi, x, 1 - core, y, z_lo)
+    row_to = lax.rem(jnp.where(c < 4, r + 1, r + 31), 32)
+    row_from = lax.rem(jnp.where(c < 4, r + 31, r + 1), 32)
+    col_to = lax.rem(jnp.where(r < 16, c + 1, c + 7), 8)
+    col_from = lax.rem(jnp.where(r < 16, c + 7, c + 1), 8)
+
+    def plane(t):
+        other = lax.rem(a + t, 16)
+        return other, device_at(z_hi, other // 4, core, lax.rem(other, 4), z_lo)
+
+    def along_z(t):
+        other = lax.rem(z + t, 8)
+        return device_at(other // 2, x, core, y, lax.rem(other, 2))
+
+    barrier = pltpu.get_barrier_semaphore()
+    signal(barrier, sibling)
+
+    @pl.loop(1, 16)
+    def _(t):
+        signal(barrier, plane(t)[1])
+
+    @pl.loop(1, 8)
+    def _(t):
+        signal(barrier, along_z(t))
+
+    signal(barrier, (row_from, c))
+    signal(barrier, (r, col_from))
+    pl.semaphore_wait(barrier, 1 + 15 + 7 + 2)
+
+    push(g_ref.at[1 - core], g0, ssem.at[0], rsem.at[0], sibling)
+    push(c_ref.at[1 - core], c0, ssem.at[1], rsem.at[1], sibling)
+    await_bytes(g0, rsem.at[0])
+    red[...] = g_ref[core] + g0[...]
+
+    @pl.loop(1, 16)
+    def _(t):
+        other, target = plane(t)
+        push(red.at[other], g1.at[t], ssem.at[2], rsem.at[2], target)
+
+    await_bytes(c0, rsem.at[1])
+    c0[...] = c0[...] + c_ref[core]
+    for t in range(1, 4):
+        x_to = lax.rem(x + t, 4)
+        push(c0.at[x_to], c1.at[t], ssem.at[3], rsem.at[3], device_at(z_hi, x_to, core, y, z_lo))
+        y_to = lax.rem(y + t, 4)
+        push(r_ref.at[y_to], r1.at[t], ssem.at[4], rsem.at[4], device_at(z_hi, x, core, y_to, z_lo))
+    await_bytes(c1.at[pl.ds(1, 3)], rsem.at[3])
+    await_bytes(r1.at[pl.ds(1, 3)], rsem.at[4])
+    c1[0] = c0[x] + c1[1] + c1[2] + c1[3]
+    r1[0] = r_ref[y] + r1[1] + r1[2] + r1[3]
+    await_bytes(g1.at[pl.ds(1, 15)], rsem.at[2])
+    gz[z] = red[a] + jnp.sum(g1[1:16], axis=0)
+
+    @pl.loop(1, 8)
+    def _(t):
+        push(gz.at[z], gz.at[z], ssem.at[5], rsem.at[5], along_z(t))
+
+    for t in range(1, 4):
+        z_to = lax.rem(z_hi + t, 4)
+        push(c1.at[0, z_to], c2.at[t], ssem.at[6], rsem.at[6], device_at(z_to, x, core, y, z_lo))
+    push(r1.at[0, 1 - z_lo], r2.at[1], ssem.at[7], rsem.at[7], device_at(z_hi, x, core, y, 1 - z_lo))
+    await_bytes(c2.at[pl.ds(1, 3)], rsem.at[6])
+    await_bytes(r2.at[1], rsem.at[7])
+    c2[0] = c1[0, z_hi] + c2[1] + c2[2] + c2[3]
+    r2[0] = r1[0, z_lo] + r2[1]
+    push(r2.at[0], r2.at[2], ssem.at[8], rsem.at[8], (row_to, c))
+    push(c2.at[0], halo, ssem.at[9], rsem.at[9], (r, col_to))
+    await_bytes(gz.at[pl.ds(0, 7)], rsem.at[5])
+    out_ref[core, a] = jnp.sum(gz[...], axis=0)
+
+    @pl.loop(1, 16)
+    def _(t):
+        push(out_ref.at[core, a], out_ref.at[core, a], ssem.at[10], rsem.at[10], plane(t)[1])
+
+    await_bytes(r2.at[2], rsem.at[8])
+    await_bytes(halo, rsem.at[9])
+    drow_ref[...] = r2[0, :, 0:64] + r2[2, :, 64:128]
+    dcol_ref[...] = c2[0, :, 0:64] + halo[:, 64:128]
+    await_bytes(out_ref.at[core, pl.ds(0, 15)], rsem.at[10])
+    push(out_ref.at[core], out_ref.at[core], ssem.at[11], rsem.at[11], sibling)
+    await_bytes(out_ref.at[0], rsem.at[11])
+
+    await_bytes(g0, ssem.at[0])
+    await_bytes(c0, ssem.at[1])
+    await_bytes(g1.at[pl.ds(1, 15)], ssem.at[2])
+    await_bytes(c1.at[pl.ds(1, 3)], ssem.at[3])
+    await_bytes(r1.at[pl.ds(1, 3)], ssem.at[4])
+    await_bytes(gz.at[pl.ds(0, 7)], ssem.at[5])
+    await_bytes(c2.at[pl.ds(1, 3)], ssem.at[6])
+    await_bytes(r2.at[1], ssem.at[7])
+    await_bytes(r2.at[2], ssem.at[8])
+    await_bytes(halo, ssem.at[9])
+    await_bytes(out_ref.at[core, pl.ds(0, 15)], ssem.at[10])
+    await_bytes(out_ref.at[0], ssem.at[11])
+
+
+def reduce_all(g, c, r):
+    vm = pl.BlockSpec(memory_space=VMEM)
+    f32 = jnp.float32
+    return pl.pallas_call(
+        reduce_kernel,
+        out_shape=(
+            jax.ShapeDtypeStruct((2, 16, 40, 128), f32),
+            jax.ShapeDtypeStruct((2, 64), f32),
+            jax.ShapeDtypeStruct((8, 64), f32),
+        ),
+        in_specs=[vm] * 3,
+        out_specs=(vm,) * 3,
+        scratch_shapes=[
+            VMEM((16, 40, 128), f32),
+            VMEM((16, 40, 128), f32),
+            VMEM((8, 40, 128), f32),
+            VMEM((4, 4, 8, 128), f32),
+            VMEM((4, 4, 8, 128), f32),
+            VMEM((4, 8, 128), f32),
+            VMEM((4, 2, 2, 128), f32),
+            VMEM((3, 2, 128), f32),
+            VMEM((16, 40, 128), f32),
+            VMEM((8, 128), f32),
+            pltpu.SemaphoreType.DMA((12,)),
+            pltpu.SemaphoreType.DMA((12,)),
+        ],
+        compiler_params=pltpu.CompilerParams(
+            collective_id=2, has_side_effects=True, vmem_limit_bytes=40 << 20
+        ),
+        name="reduce_all",
+    )(g, c, r)
 
 
 def project(features, weight):
@@ -135,6 +363,16 @@
             )
         stacked.append(jnp.stack(line_list))
     return jnp.stack(stacked)
+
+
+def live_cells(first_cell, count, cell_limit):
+    cells = first_cell + lax.broadcasted_iota(jnp.int32, (count, 256), 0)
+    return (cells >= 0) & (cells < cell_limit)
+
+
+def placed(value, offset, count):
+    zeros = jnp.zeros((count, value.shape[1]), value.dtype)
+    return lax.dynamic_update_slice_in_dim(zeros, value, offset, 0)
 
 
 def shards(
@@ -161,13 +399,16 @@
     col_start = col_place * cols_here
     row_limit = rows_here * row_count
     col_limit = cols_here * col_count
-    row_piece = row_features.shape[0]
-    col_piece = col_features.shape[0]
-    rows_a = gathered_copies(project(row_features, row_proj), "col", 0)
-    cols_b = gathered_copies(project(col_features, col_proj), "row", 0)
     pad_reach = 2 * margin
-    a_pad = padded_2(rows_a, (("row", 0),), 2 * MAX_DILATION)
-    b_pad = padded_2(cols_b, (("col", 0),), 2 * MAX_DILATION)
+    cot_t = jnp.swapaxes(cotangent, 0, 1)
+    cf = jnp.concatenate([col_features[:, :128], col_features[:, 128:]], axis=0)
+    row_f, col_f, halo, side = gather_all(row_features.astype(jnp.float32), cf, cot_t)
+    row_f = row_f.reshape(48, 256)
+    row_f = jnp.where(live_cells(row_start - pad_reach, 48, row_limit), row_f, 0.0).astype(jnp.bfloat16)
+    col_f = jnp.concatenate([col_f[:, :8], col_f[:, 8:]], axis=2).reshape(288, 256)
+    col_f = jnp.where(live_cells(col_start - pad_reach, 288, col_limit), col_f, 0)
+    a_pad = project(row_f, row_proj)
+    b_pad = project(col_f, col_proj)
     row_terms = line_terms(
         a_pad, pair_weight[0], first_rate, rows_here + 2 * margin, pad_reach - margin
     )
@@ -190,7 +431,12 @@
     hidden_own = hidden[:, margin : margin + rows_here, margin : margin + cols_here]
     conv_mixed = conv_taps(hidden, conv_weight, second_rate, rows_here, cols_here, margin)
     pair_out = (hidden_own.astype(jnp.float32) + conv_mixed).astype(jnp.bfloat16)
-    grad_pad = padded_2(cotangent, (("row", 1), ("col", 2)), MAX_DILATION)
+    side = side.reshape(2, 3, 64, 16, 8)
+    side = jnp.concatenate([side[:, 0, :, 8:], side[:, 1], side[:, 2, :, :8]], axis=2)
+    halo = jnp.moveaxis(halo, 2, 1)
+    grad_pad = jnp.concatenate([halo[0], cotangent, halo[1]], axis=1)
+    grad_pad = jnp.concatenate([side[0], grad_pad, side[1]], axis=2)
+    grad_pad = jnp.where(row_inside[None, :, None] * col_inside[None, None, :] > 0, grad_pad, 0)
     d_hidden = cotangent.astype(jnp.float32) + back_taps(
         grad_pad, conv_weight, second_rate, rows_here, cols_here, margin
     )
@@ -202,95 +448,59 @@
     col_valid_own = line_valid(col_start, cols_here, col_limit, first_rate)
     row_part = jnp.einsum("jq,cij->qic", col_valid_own, d_pre, precision=lax.Precision.HIGHEST)
     col_part = jnp.einsum("ik,cij->kjc", row_valid_own, d_pre, precision=lax.Precision.HIGHEST)
-    row_sums = over_copies(row_part, "col")
-    col_sums = total_of_pieces(col_part, "row")
-    back_rows = jnp.einsum(
-        "qio,kqpo->kip",
-        row_sums,
-        pair_weight[0].astype(jnp.float32),
-        precision=lax.Precision.HIGHEST,
-    )
-    back_cols = jnp.einsum(
-        "kjo,kqpo->qjp",
-        col_sums,
-        pair_weight[1].astype(jnp.float32),
-        precision=lax.Precision.HIGHEST,
-    )
-    rows_back_pad = padded_2(back_rows, (("row", 1),), MAX_DILATION)
-    cols_back_pad = padded_2(back_cols, (("col", 1),), MAX_DILATION)
-    row_own = col_place * row_piece
-    col_own = row_place * col_piece
-    d_rows = sum(
-        (
-            lax.dynamic_slice_in_dim(
-                rows_back_pad[tap_idx], margin + row_own - (tap_idx - 1) * first_rate, row_piece, 0
-            )
-            for tap_idx in range(3)
-        )
-    )
-    d_cols = sum(
-        (
-            lax.dynamic_slice_in_dim(
-                cols_back_pad[tap_idx], margin + col_own - (tap_idx - 1) * first_rate, col_piece, 0
-            )
-            for tap_idx in range(3)
-        )
-    )
-    d_rows = d_rows.astype(jnp.bfloat16)
-    d_cols = d_cols.astype(jnp.bfloat16)
+    high = lax.Precision.HIGHEST
+    pair_wide = pair_weight.astype(jnp.float32)
+    back_rows = jnp.einsum("qio,kqpo->kip", row_part, pair_wide[0], precision=high)
+    back_cols = jnp.einsum("kjo,kqpo->qjp", col_part, pair_wide[1], precision=high)
+    d_rows = sum(placed(back_rows[k], margin + (k - 1) * first_rate, rows_here + 2 * margin) for k in range(3))
+    d_cols = sum(placed(back_cols[k], margin + (k - 1) * first_rate, cols_here + 2 * margin) for k in range(3))
+    d_rows = jnp.where(row_inside[:, None] > 0, d_rows, 0.0)
+    d_cols = jnp.where(col_inside[:, None] > 0, d_cols, 0.0)
+    row_mid = row_f[margin : margin + 32].astype(jnp.float32)
+    col_mid = col_f[margin : margin + 272].astype(jnp.float32)
+    grad_row_proj = jnp.einsum("ic,ip->cp", row_mid, d_rows, precision=high)
+    grad_col_proj = jnp.einsum("ic,ip->cp", col_mid, d_cols, precision=high)
+    row_shifted = jnp.stack(
+        [lax.dynamic_slice_in_dim(a_pad, pad_reach + (k - 1) * first_rate, rows_here, 0) for k in range(3)]
+    ).astype(jnp.float32)
+    col_shifted = jnp.stack(
+        [lax.dynamic_slice_in_dim(b_pad, pad_reach + (k - 1) * first_rate, cols_here, 0) for k in range(3)]
+    ).astype(jnp.float32)
+    grad_row_pair = jnp.einsum("kip,qio->kqpo", row_shifted, row_part, precision=high)
+    grad_col_pair = jnp.einsum("qjp,kjo->kqpo", col_shifted, col_part, precision=high)
+    flat = [
+        grad_row_proj.reshape(-1),
+        grad_col_proj.reshape(-1),
+        grad_row_pair.reshape(-1),
+        grad_col_pair.reshape(-1),
+        conv_grad.reshape(-1),
+        bias_grad,
+    ]
+    packed = jnp.concatenate(flat)
+    packed = jnp.pad(packed, (0, 163840 - packed.shape[0])).reshape(2, 16, 40, 128)
+    main_c = d_cols[8:264].reshape(32, 8, 64)
+    zero = jnp.zeros((30, 8, 64), jnp.float32)
+    halo_c = jnp.concatenate([d_cols[None, 264:272], zero, d_cols[None, 0:8]])
+    pieces_c = jnp.concatenate([main_c, halo_c], axis=2).reshape(4, 4, 2, 8, 128)
+    pieces_c = jnp.transpose(pieces_c, (2, 1, 0, 3, 4))
+    main_r = d_rows[8:24].reshape(8, 2, 64)
+    halo_r = jnp.concatenate([d_rows[24:32], d_rows[0:8]]).reshape(8, 2, 64)
+    pieces_r = jnp.concatenate([main_r, halo_r], axis=2).reshape(4, 2, 2, 128)
+    total, own_rows, own_cols = reduce_all(packed, pieces_c, pieces_r)
+    d_rows = own_rows.astype(jnp.bfloat16)
+    d_cols = own_cols.astype(jnp.bfloat16)
     grad_row_features = jnp.dot(d_rows, row_proj.T, preferred_element_type=jnp.float32)
     grad_col_features = jnp.dot(d_cols, col_proj.T, preferred_element_type=jnp.float32)
-    grad_row_proj = jnp.dot(row_features.T, d_rows, preferred_element_type=jnp.float32)
-    grad_col_proj = jnp.dot(col_features.T, d_cols, preferred_element_type=jnp.float32)
-    row_shifted = jnp.stack(
-        [
-            lax.dynamic_slice_in_dim(
-                a_pad, pad_reach + row_own + (tap_idx - 1) * first_rate, row_piece, 0
-            )
-            for tap_idx in range(3)
-        ]
-    )
-    col_shifted = jnp.stack(
-        [
-            lax.dynamic_slice_in_dim(
-                b_pad, pad_reach + col_own + (tap_idx - 1) * first_rate, col_piece, 0
-            )
-            for tap_idx in range(3)
-        ]
-    )
-    row_sums_own = lax.dynamic_slice_in_dim(row_sums, row_own, row_piece, 1)
-    col_sums_own = lax.dynamic_slice_in_dim(col_sums, col_own, col_piece, 1)
-    grad_row_pair = jnp.einsum(
-        "kip,qio->kqpo",
-        row_shifted.astype(jnp.float32),
-        row_sums_own,
-        precision=lax.Precision.HIGHEST,
-    )
-    grad_col_pair = jnp.einsum(
-        "qjp,kjo->kqpo",
-        col_shifted.astype(jnp.float32),
-        col_sums_own,
-        precision=lax.Precision.HIGHEST,
-    )
-    summed = lax.psum(
-        (
-            grad_row_proj,
-            grad_col_proj,
-            jnp.stack([grad_row_pair, grad_col_pair]),
-            bias_grad,
-            conv_grad,
-        ),
-        ("row", "col"),
-    )
+    total = total.reshape(-1)
     return (
         pair_out,
         grad_row_features,
         grad_col_features,
-        summed[0],
-        summed[1],
-        summed[2],
-        summed[3],
-        summed[4],
+        total[:16384].reshape(256, 64),
+        total[16384:32768].reshape(256, 64),
+        total[32768:106496].reshape(2, 3, 3, 64, 64),
+        total[143360:143424],
+        total[106496:143360].reshape(3, 3, 64, 64),
     )
 
 

time: 498 us -> 128 us (0.26)
  waiting for transfers between devices: 280 us -> 0 us
  blocking collectives: 78 us -> 0 us
  starting transfers between devices: 57.2 us -> 0 us
  Pallas kernels: 0 us -> 56.9 us
  between operations: 24.8 us -> 12.2 us
  matrix products: 29 us -> 37.1 us
  other arithmetic: 12.7 us -> 7 us
    psum x1 -> x0, waiting for transfers between devices: 254 us -> none  [shards(): lax.psum((grad_row_proj, grad_col_proj, jnp.stack([grad_row_pair, grad_co...]
    psum x1 -> x0, blocking collectives: 78 us -> none  [shards(): lax.psum((grad_row_proj, grad_col_proj, jnp.stack([grad_row_pair, grad_co...]
    pallas_call x0 -> x2, Pallas kernels: none -> 56.9 us  [the longest x1 30.1 us: reduce_all(): pl.pallas_call(reduce_kernel, out_shape=(jax.ShapeDtypeStruct((2, 16, 40,...]
    ppermute x12 -> x0, starting transfers between devices: 34.1 us -> none  [the longest x6 24.3 us: padded_2(): before = lax.ppermute(last, axis, up)]
    all_to_all x3 -> x0, starting transfers between devices: 23 us -> none  [sent_to_all(): return lax.all_to_all(copies, axis, split_axis=0, concat_axis=0, tiled=True)]
    ppermute x12 -> x0, waiting for transfers between devices: 21.2 us -> none  [the longest x6 17.4 us: padded_2(): after = lax.ppermute(leading, axis, down)]
  transfers between devices with their start and end apart: 17 -> 0, of which waited for: 6 -> 0; matrix products, arithmetic and copies ran while one was open for 7% -> 0% of each run, Pallas kernels for 0% -> 0%
where the time goes in v1:
time: 128 us; the launch traced here: 127 us
  Pallas kernels  56.9 us (44%)
  matrix products  37.1 us (29%)
  local copies, waits for them, and re-layouts  13.7 us (11%)
  between operations  12.2 us (10%)
  other arithmetic  7 us (5%)
    pallas_call x1, Pallas kernels, reduce_all(): pl.pallas_call(reduce_kernel, out_shape=(jax.ShapeDtypeStruct((2, 16, 40,...  30.1 us
    pallas_call x1, Pallas kernels, gather_all(): pl.pallas_call(gather_kernel, out_shape=(jax.ShapeDtypeStruct((3, 8, 2, 2...  26.9 us
    dot_general x9, matrix products, conv_taps(): jnp.einsum('co,cij->oij', weight[tap_row, tap_col], window, preferred_ele...  8.06 us
    dot_general x1, matrix products, pair_field(): jnp.einsum('jq,qic->cij', col_valid, row_terms, precision=lax.Precision.H...  7.89 us
    dot_general x9, matrix products, tap_grads(): jnp.einsum('cij,oij->co', window, grads, preferred_element_type=jnp.float32)  6.12 us
    dot_general x9, matrix products, back_taps(): jnp.einsum('co,oij->cij', weight[tap_row, tap_col], window, preferred_ele...  6.11 us
    unnamed x38, local copies, waits for them, and re-layouts  5.17 us
    dot_general x1, matrix products, pair_field(): jnp.einsum('ik,kjc->cij', row_valid, col_terms, precision=lax.Precision.H...  3.13 us

profile of v1, /device:TPU:1, one launch (start us, length us, event | category | flops | bytes accessed | tf_op | source)
XLA Modules:
  0.0 126.9 jit_solution(219391812162271744)
XLA Ops:
  0.7 0.7 convert_element_type.63.rf_ref
  2.1 1.2 copy.267
  3.3 26.9 %gather_all.1 = (f32[3,8,2,256]{3,2,1,0:T(2,128)S(1)}, bf16[36,16,128]{2,1,0:T(8,128)(2,1)S(1)}, bf16[2,8,64,256]{3,2,1,0:T(8,128)(2,1)S(1)}, bf16[2,3,64,128]{3,2,1,0:T(8,128)(2,1)S(1)}) custom-call(f32[2,256]{1,0:T(2,128)S(1)} %convert_element_type.63.rf_ref, bf16[16,128]{1,0:T(8,128)(2,1)S(1)} %pad_maximum_fusion.6.cf_ref, bf16[16,64,256]{2,1,0:T(8,128)(2,1)S(1)} %bitcast.332), custom_call_target="tpu_custom_call" | custom-call | tf_op jit(solution)/shard_map/gather_all/pallas_call | solution.py:118
  34.4 3.1 %fusion.39 = f32[272,64,32]{0,2,1:T(8,128)} fusion(f32[3,272,64]{1,2,0:T(8,128)S(1)} %convolution_bitcast_fusion.1, pred[32,1]{0,1:T(4,128)(4,1)S(1)} %get-tuple-element.94, pred[32,1]{0,1:T(4,128)(4,1)S(1)} %get-tuple-element.95, pred[32,1]{0,1:T(4,128)(4,1)S(1)} %compare_and_fusion.11), kind=kOutput, calls=%fused_computation.75 | convolution fusion | flops 20054208 | bytes 2437216 | tf_op jit(solution)/shard_map/ik,kjc->cij/dot_general | solution.py:306
  39.4 7.9 %multiply_convert_fusion = (bf16[64,32,272]{2,0,1:T(8,128)(2,1)S(1)}, f32[64,32,272]{2,0,1:T(8,128)}) fusion(f32[272]{0:T(512)S(1)} %get-tuple-element.88, f32[32]{0:T(128)S(1)} %get-tuple-element.92, f32[64]{0:T(128)S(1)} %copy-done.12, f32[272,64,32]{0,2,1:T(8,128)} %fusion.39, pred[272,1]{0,1:T(4,128)(4,1)S(1)} %get-tuple-element.84, ...), kind=kOutput, calls=%fused_computation.2 | convolution fusion | flops 25069152 | bytes 5597424 | tf_op jit(solution)/shard_map/jq,qic->cij/dot_general | solution.py:305
  48.3 1.4 %convolution_add_fusion.15 = f32[16,256,64]{1,2,0:T(8,128)} fusion(f32[16,256,64]{1,2,0:T(8,128)S(1)} %fusion.35, bf16[64,32,272]{2,0,1:T(8,128)(2,1)S(1)} %get-tuple-element.80, s32[]{:T(128)S(6)} %select_n.114, bf16[3,3,64,64]{3,2,1,0:T(8,128)(2,1)S(1)} %copy-done.5), kind=kOutput, calls=%fused_computation.25 | convolution fusion | flops 33816576 | bytes 2637828 | tf_op jit(solution)/shard_map/co,cij->oij/dot_general | solution.py:326
  51.0 1.6 %convolution_add_fusion.14 = f32[16,256,64]{1,2,0:T(8,128)S(1)} fusion(f32[16,256,64]{1,2,0:T(8,128)} %convolution_add_fusion.15, bf16[64,32,272]{2,0,1:T(8,128)(2,1)S(1)} %get-tuple-element.80, s32[]{:T(128)S(6)} %select_n.114, s32[]{:T(128)S(6)} %select_n.116, bf16[3,3,64,64]{3,2,1,0:T(8,128)(2,1)S(1)} %copy-done.5), kind=kOutput, calls=%fused_computation.24 | convolution fusion | flops 33816576 | bytes 2637832 | tf_op jit(solution)/shard_map/co,cij->oij/dot_general | solution.py:326
  53.5 1.4 %convolution_add_fusion.11 = f32[16,256,64]{1,2,0:T(8,128)} fusion(f32[16,256,64]{1,2,0:T(8,128)S(1)} %convolution_add_fusion.12, bf16[64,32,272]{2,0,1:T(8,128)(2,1)S(1)} %get-tuple-element.80, s32[]{:T(128)S(6)} %select_n.116, bf16[3,3,64,64]{3,2,1,0:T(8,128)(2,1)S(1)} %copy-done.5), kind=kOutput, calls=%fused_computation.21 | convolution fusion | flops 33816576 | bytes 2637828 | tf_op jit(solution)/shard_map/co,cij->oij/dot_general | solution.py:326
  55.5 1.6 %convolution_add_fusion.10 = f32[16,256,64]{1,2,0:T(8,128)S(1)} fusion(f32[16,256,64]{1,2,0:T(8,128)} %convolution_add_fusion.11, bf16[64,32,272]{2,0,1:T(8,128)(2,1)S(1)} %get-tuple-element.80, s32[]{:T(128)S(6)} %select_n.117, s32[]{:T(128)S(6)} %select_n.115, bf16[3,3,64,64]{3,2,1,0:T(8,128)(2,1)S(1)} %copy-done.5), kind=kOutput, calls=%fused_computation.20 | convolution fusion | flops 33816576 | bytes 2637832 | tf_op jit(solution)/shard_map/co,cij->oij/dot_general | solution.py:326
  58.0 1.1 copy.171
  59.7 0.8 slice_bitcast_fusion.1
  60.8 2.6 %maximum_select_fusion = bf16[64,32,272]{2,0,1:T(8,128)(2,1)S(1)} fusion(bf16[64,32,8]{2,0,1:T(8,128)(2,1)S(1)} %bitcast.338, bf16[64,8,256]{2,0,1:T(8,128)(2,1)} %get-tuple-element.49, bf16[64,16,256]{2,0,1:T(8,128)(2,1)S(1)} %copy.267, bf16[64,8,256]{2,0,1:T(8,128)(2,1)} %get-tuple-element.48, bf16[64,32,8]{2,0,1:T(8,128)(2,1)S(1)} %bitcast.339, ...), kind=kLoop, calls=%fused_computation.3 | loop fusion | flops 6127616 | bytes 2236928 | tf_op jit(solution)/shard_map/jit(_where)/select_n | solution.py:439
  63.5 1.1 fusion.18
  69.9 2.4 %fusion.205 = (f32[64]{0:T(128)S(1)}, f32[64,16,256]{2,0,1:T(8,128)S(1)}) fusion(f32[64,32,272]{2,0,1:T(8,128)} %get-tuple-element.81, f32[16,256,64]{1,2,0:T(8,128)S(1)} %convolution_add_fusion.1, bf16[64,32,272]{2,0,1:T(8,128)(2,1)S(1)} %maximum_select_fusion, s32[]{:T(128)S(6)} %select_n.122, s32[]{:T(128)S(6)} %select_n.121, ...), kind=kOutput, calls=%fused_computation.320 | convolution fusion | flops 36700096 | bytes 4210952 | tf_op jit(solution)/shard_map/co,oij->cij/dot_general | solution.py:343
  73.0 0.7 fusion.142
  76.3 1.1 fusion.8
  79.1 0.9 add.648
  84.1 1.5 %convolution_bitcast_fusion.5 = f32[1,64,64]{2,1,0:T(8,128)S(1)} fusion(bf16[64,32,272]{2,0,1:T(8,128)(2,1)S(1)} %copy-done.2, s32[]{:T(128)S(6)} %select_n.117, s32[]{:T(128)S(6)} %select_n.116, bf16[64,16,256]{2,1,0:T(8,128)(2,1)} %param.17), kind=kOutput, calls=%fused_computation.33 | convolution fusion | flops 33554432 | bytes 1064968 | tf_op jit(solution)/shard_map/cij,oij->co/dot_general | solution.py:362
  85.6 1.5 %convolution_bitcast_fusion.6 = f32[1,64,64]{2,1,0:T(8,128)S(1)} fusion(bf16[64,32,272]{2,0,1:T(8,128)(2,1)S(1)} %copy-done.2, s32[]{:T(128)S(6)} %select_n.117, bf16[64,16,256]{2,1,0:T(8,128)(2,1)} %param.17), kind=kOutput, calls=%fused_computation.34 | convolution fusion | flops 33554432 | bytes 1064964 | tf_op jit(solution)/shard_map/cij,oij->co/dot_general | solution.py:362
  91.4 30.1 %reduce_all.1 = (f32[2,16,40,128]{3,2,1,0:T(8,128)S(1)}, f32[2,64]{1,0:T(2,128)S(1)}, f32[8,64]{1,0:T(8,128)S(1)}) custom-call(f32[2,16,40,128]{3,2,1,0:T(8,128)S(1)} %bitcast.333, f32[2,4,4,8,128]{4,3,2,1,0:T(8,128)S(1)} %copy_bitcast_fusion.2.c_ref, f32[4,2,2,128]{3,2,1,0:T(2,128)S(1)} %pad_maximum_fusion.5.r_ref), custom_call_target="tpu_custom_call" | custom-call | tf_op jit(solution)/shard_map/reduce_all/pallas_call | solution.py:246
  122.1 0.7 fusion.147
  123.1 0.7 copy.172
  124.6 1.0 reshape.315
  126.1 0.8 reshape.316
  (139 shorter events, 21.8 us)
Async XLA Ops:
  0.6 29.7 %copy-start = (bf16[256,64]{0,1:T(8,128)(2,1)S(1)}, bf16[256,64]{0,1:T(8,128)(2,1)}, u32[]{:S(2)}) copy-start(bf16[256,64]{0,1:T(8,128)(2,1)} %param.12) | copy-start | bytes 98308
  0.6 29.9 %copy-start.11 = (s32[2]{0:T(128)S(1)}, s32[2]{0:T(128)}, u32[]{:S(2)}) copy-start(s32[2]{0:T(128)} %param.16) | copy-start | bytes 28
  0.7 32.6 %copy-start.3 = (bf16[2,3,3,64,64]{4,3,2,1,0:T(8,128)(2,1)S(1)}, bf16[2,3,3,64,64]{4,3,2,1,0:T(8,128)(2,1)}, u32[]{:S(2)}) copy-start(bf16[2,3,3,64,64]{4,3,2,1,0:T(8,128)(2,1)} %param.13) | copy-start | bytes 442372
  34.4 4.0 %copy-start.9 = (bf16[256,64]{0,1:T(8,128)(2,1)S(1)}, bf16[256,64]{0,1:T(8,128)(2,1)}, u32[]{:S(2)}) copy-start(bf16[256,64]{0,1:T(8,128)(2,1)} %param.11) | copy-start | bytes 98308
  34.4 5.0 %copy-start.12 = (f32[64]{0:T(128)S(1)}, f32[64]{0:T(128)}, u32[]{:S(2)}) copy-start(f32[64]{0:T(128)} %param.14) | copy-start | bytes 772
  39.4 8.6 %copy-start.5 = (bf16[3,3,64,64]{3,2,1,0:T(8,128)(2,1)S(1)}, bf16[3,3,64,64]{3,2,1,0:T(8,128)(2,1)}, u32[]{:S(2)}) copy-start(bf16[3,3,64,64]{3,2,1,0:T(8,128)(2,1)} %param.15) | copy-start | bytes 221188
  47.3 10.3 %copy-start.1 = (bf16[64,32,272]{2,0,1:T(8,128)(2,1)}, bf16[64,32,272]{2,0,1:T(8,128)(2,1)S(1)}, u32[]{:S(2)}) copy-start(bf16[64,32,272]{2,0,1:T(8,128)(2,1)S(1)} %get-tuple-element.80) | copy-start | bytes 3342340
  63.5 1.2 copy-start.6
  68.9 1.0 copy-start.7
  69.9 3.8 %copy-start.4 = (bf16[2,3,3,64,64]{4,3,2,1,0:T(8,128)(2,1)S(1)}, bf16[2,3,3,64,64]{4,3,2,1,0:T(8,128)(2,1)}, u32[]{:S(2)}) copy-start(bf16[2,3,3,64,64]{4,3,2,1,0:T(8,128)(2,1)} %param.13) | copy-start | bytes 442372
  82.4 1.6 %copy-start.2 = (bf16[64,32,272]{2,0,1:T(8,128)(2,1)S(1)}, bf16[64,32,272]{2,0,1:T(8,128)(2,1)}, u32[]{:S(2)}) copy-start(bf16[64,32,272]{2,0,1:T(8,128)(2,1)} %copy-done.1) | copy-start | bytes 3342340
  84.0 3.1 %copy-start.8 = (bf16[64,16,256]{2,1,0:T(8,128)(2,1)S(1)}, bf16[64,16,256]{2,1,0:T(8,128)(2,1)}, u32[]{:S(2)}) copy-start(bf16[64,16,256]{2,1,0:T(8,128)(2,1)} %param.17) | copy-start | bytes 1572868
  90.5 30.9 %copy-start.10 = (bf16[256,64]{0,1:T(8,128)(2,1)S(1)}, bf16[256,64]{0,1:T(8,128)(2,1)}, u32[]{:S(2)}) copy-start(bf16[256,64]{0,1:T(8,128)(2,1)} %param.11) | copy-start | bytes 98308

commit v2 on v1

v2 whole, which is shorter than its diff:
```python
import functools

import jax
import jax.numpy as jnp
from jax import lax
from jax.experimental import pallas as pl
from jax.experimental.pallas import tpu as pltpu
from jax.sharding import PartitionSpec as P

MAX_DILATION = 8
MESH = pl.DeviceIdType.MESH
VMEM = pltpu.VMEM


def places():
    r = lax.axis_index("row")
    c = lax.axis_index("col")
    return r, c, r // 8, lax.rem(r // 2, 4), lax.rem(r, 2), c // 2, lax.rem(c, 2)


def device_at(z_hi, x, core, y, z_lo):
    return ((z_hi * 4 + x) * 2 + core, y * 2 + z_lo)


def signal(barrier, target):
    pl.semaphore_signal(barrier, inc=1, device_id=target, device_id_type=MESH)


def push(src, dst, send_sem, recv_sem, target):
    pltpu.make_async_remote_copy(
        src_ref=src,
        dst_ref=dst,
        send_sem=send_sem,
        recv_sem=recv_sem,
        device_id=target,
        device_id_type=MESH,
    ).start()


def await_bytes(ref, sem):
    pltpu.make_async_copy(ref, ref, sem).wait()


def gather_kernel(rf_ref, cf_ref, cot_ref, rows_ref, cols_ref, halo_ref, side_ref, pack, ssem, rsem):
    r, c, _, _, _, _, _ = places()
    up, down = lax.rem(r + 31, 32), lax.rem(r + 1, 32)
    left, right = lax.rem(c + 7, 8), lax.rem(c + 1, 8)
    barrier = pltpu.get_barrier_semaphore()

    @pl.loop(1, 32)
    def _(t):
        signal(barrier, (lax.rem(r + t, 32), c))

    @pl.loop(1, 8)
    def _(t):
        signal(barrier, (r, lax.rem(c + t, 8)))

    for r_to in (up, down):
        for c_to in (left, right):
            signal(barrier, (r_to, c_to))

    lane = lax.broadcasted_iota(jnp.int32, (64, 128), 1) // 8
    first = jnp.zeros((64, 128), jnp.float32)
    last = jnp.zeros((64, 128), jnp.float32)
    for i in range(16):
        head = cot_ref[i, :, 0:128].astype(jnp.float32)
        tail = cot_ref[i, :, 128:256].astype(jnp.float32)
        first = jnp.where(lane == i, pltpu.roll(head, 8 * i, 1) if i else head, first)
        last = jnp.where(lane == i, pltpu.roll(tail, (8 * i + 8) % 128, 1) if i < 15 else tail, last)
    pack[0] = first.astype(jnp.bfloat16)
    pack[1] = last.astype(jnp.bfloat16)
    rows_ref[1, c] = rf_ref[...]
    cols_ref[r + 2] = cf_ref[...]
    pl.semaphore_wait(barrier, 31 + 7 + 4)

    push(cot_ref.at[pl.ds(8, 8)], halo_ref.at[0], ssem.at[0], rsem.at[0], (down, c))
    push(cot_ref.at[pl.ds(0, 8)], halo_ref.at[1], ssem.at[1], rsem.at[1], (up, c))

    @pl.loop(1, 32)
    def _(t):
        push(cf_ref, cols_ref.at[r + 2], ssem.at[2], rsem.at[2], (lax.rem(r + t, 32), c))

    @pl.loop(1, 8)
    def _(t):
        push(rf_ref, rows_ref.at[1, c], ssem.at[3], rsem.at[3], (r, lax.rem(c + t, 8)))

    for slot, r_to in ((2, up), (1, r), (0, down)):
        push(pack.at[0], side_ref.at[1, slot], ssem.at[4], rsem.at[4], (r_to, left))
        push(pack.at[1], side_ref.at[0, slot], ssem.at[4], rsem.at[4], (r_to, right))

    await_bytes(rows_ref.at[1, pl.ds(0, 7)], rsem.at[3])
    push(rows_ref.at[1], rows_ref.at[0], ssem.at[5], rsem.at[5], (down, c))
    push(rows_ref.at[1], rows_ref.at[2], ssem.at[6], rsem.at[6], (up, c))
    await_bytes(cols_ref.at[pl.ds(2, 31)], rsem.at[2])
    push(cols_ref.at[pl.ds(2, 2)], cols_ref.at[pl.ds(34, 2)], ssem.at[7], rsem.at[7], (r, left))
    push(cols_ref.at[pl.ds(32, 2)], cols_ref.at[pl.ds(0, 2)], ssem.at[8], rsem.at[8], (r, right))

    await_bytes(halo_ref.at[0], rsem.at[0])
    await_bytes(halo_ref.at[1], rsem.at[1])
    await_bytes(side_ref, rsem.at[4])
    await_bytes(rows_ref.at[0], rsem.at[5])
    await_bytes(rows_ref.at[2], rsem.at[6])
    await_bytes(cols_ref.at[pl.ds(34, 2)], rsem.at[7])
    await_bytes(cols_ref.at[pl.ds(0, 2)], rsem.at[8])
    await_bytes(halo_ref.at[0], ssem.at[0])
    await_bytes(halo_ref.at[1], ssem.at[1])
    await_bytes(cols_ref.at[pl.ds(2, 31)], ssem.at[2])
    await_bytes(rows_ref.at[1, pl.ds(0, 7)], ssem.at[3])
    await_bytes(side_ref, ssem.at[4])
    await_bytes(rows_ref.at[0], ssem.at[5])
    await_bytes(rows_ref.at[2], ssem.at[6])
    await_bytes(cols_ref.at[pl.ds(34, 2)], ssem.at[7])
    await_bytes(cols_ref.at[pl.ds(0, 2)], ssem.at[8])


def gather_all(rf, cf, cot):
    vm = pl.BlockSpec(memory_space=VMEM)
    return pl.pallas_call(
        gather_kernel,
        out_shape=(
            jax.ShapeDtypeStruct((3, 8, 2, 256), jnp.float32),
            jax.ShapeDtypeStruct((36, 16, 128), jnp.bfloat16),
            jax.ShapeDtypeStruct((2, 8, 64, 256), jnp.bfloat16),
            jax.ShapeDtypeStruct((2, 3, 64, 128), jnp.bfloat16),
        ),
        in_specs=[vm] * 3,
        out_specs=(vm,) * 4,
        scratch_shapes=[
            VMEM((2, 64, 128), jnp.bfloat16),
            pltpu.SemaphoreType.DMA((9,)),
            pltpu.SemaphoreType.DMA((9,)),
        ],
        compiler_params=pltpu.CompilerParams(
            collective_id=1, has_side_effects=True, vmem_limit_bytes=40 << 20
        ),
        name="gather_all",
    )(rf, cf, cot)


def reduce_kernel(
    g_ref, c_ref, r_ref, out_ref, drow_ref, dcol_ref,
    g0, g1, gz, c0, c1, c2, r1, r2, red, halo, ssem, rsem,
):
    r, c, z_hi, x, core, y, z_lo = places()
    a = x * 4 + y
    z = z_hi * 2 + z_lo
    sibling = device_at(z_hi, x, 1 - core, y, z_lo)
    row_to = lax.rem(jnp.where(c < 4, r + 1, r + 31), 32)
    row_from = lax.rem(jnp.where(c < 4, r + 31, r + 1), 32)
    col_to = lax.rem(jnp.where(r < 16, c + 1, c + 7), 8)
    col_from = lax.rem(jnp.where(r < 16, c + 7, c + 1), 8)

    def plane(t):
        other = lax.rem(a + t, 16)
        return other, device_at(z_hi, other // 4, core, lax.rem(other, 4), z_lo)

    def along_z(t):
        other = lax.rem(z + t, 8)
        return device_at(other // 2, x, core, y, lax.rem(other, 2))

    barrier = pltpu.get_barrier_semaphore()
    signal(barrier, sibling)

    @pl.loop(1, 16)
    def _(t):
        signal(barrier, plane(t)[1])

    @pl.loop(1, 8)
    def _(t):
        signal(barrier, along_z(t))

    signal(barrier, (row_from, c))
    signal(barrier, (r, col_from))
    pl.semaphore_wait(barrier, 1 + 15 + 7 + 2)

    push(g_ref.at[1 - core], g0, ssem.at[0], rsem.at[0], sibling)
    push(c_ref.at[1 - core], c0, ssem.at[1], rsem.at[1], sibling)
    await_bytes(g0, rsem.at[0])
    red[...] = g_ref[core] + g0[...]

    @pl.loop(1, 16)
    def _(t):
        other, target = plane(t)
        push(red.at[other], g1.at[t], ssem.at[2], rsem.at[2], target)

    await_bytes(c0, rsem.at[1])
    c0[...] = c0[...] + c_ref[core]
    for t in range(1, 4):
        x_to = lax.rem(x + t, 4)
        push(c0.at[x_to], c1.at[t], ssem.at[3], rsem.at[3], device_at(z_hi, x_to, core, y, z_lo))
        y_to = lax.rem(y + t, 4)
        push(r_ref.at[y_to], r1.at[t], ssem.at[4], rsem.at[4], device_at(z_hi, x, core, y_to, z_lo))
    await_bytes(c1.at[pl.ds(1, 3)], rsem.at[3])
    await_bytes(r1.at[pl.ds(1, 3)], rsem.at[4])
    c1[0] = c0[x] + c1[1] + c1[2] + c1[3]
    r1[0] = r_ref[y] + r1[1] + r1[2] + r1[3]
    await_bytes(g1.at[pl.ds(1, 15)], rsem.at[2])
    gz[z] = red[a] + jnp.sum(g1[1:16], axis=0)

    @pl.loop(1, 8)
    def _(t):
        push(gz.at[z], gz.at[z], ssem.at[5], rsem.at[5], along_z(t))

    for t in range(1, 4):
        z_to = lax.rem(z_hi + t, 4)
        push(c1.at[0, z_to], c2.at[t], ssem.at[6], rsem.at[6], device_at(z_to, x, core, y, z_lo))
    push(r1.at[0, 1 - z_lo], r2.at[1], ssem.at[7], rsem.at[7], device_at(z_hi, x, core, y, 1 - z_lo))
    await_bytes(c2.at[pl.ds(1, 3)], rsem.at[6])
    await_bytes(r2.at[1], rsem.at[7])
    c2[0] = c1[0, z_hi] + c2[1] + c2[2] + c2[3]
    r2[0] = r1[0, z_lo] + r2[1]
    push(r2.at[0], r2.at[2], ssem.at[8], rsem.at[8], (row_to, c))
    push(c2.at[0], halo, ssem.at[9], rsem.at[9], (r, col_to))
    await_bytes(gz.at[pl.ds(0, 7)], rsem.at[5])
    out_ref[core, a] = jnp.sum(gz[...], axis=0)

    @pl.loop(1, 16)
    def _(t):
        push(out_ref.at[core, a], out_ref.at[core, a], ssem.at[10], rsem.at[10], plane(t)[1])

    await_bytes(r2.at[2], rsem.at[8])
    await_bytes(halo, rsem.at[9])
    drow_ref[...] = r2[0, :, 0:64] + r2[2, :, 64:128]
    dcol_ref[...] = c2[0, :, 0:64] + halo[:, 64:128]
    await_bytes(out_ref.at[core, pl.ds(0, 15)], rsem.at[10])
    push(out_ref.at[core], out_ref.at[core], ssem.at[11], rsem.at[11], sibling)
    await_bytes(out_ref.at[0], rsem.at[11])

    await_bytes(g0, ssem.at[0])
    await_bytes(c0, ssem.at[1])
    await_bytes(g1.at[pl.ds(1, 15)], ssem.at[2])
    await_bytes(c1.at[pl.ds(1, 3)], ssem.at[3])
    await_bytes(r1.at[pl.ds(1, 3)], ssem.at[4])
    await_bytes(gz.at[pl.ds(0, 7)], ssem.at[5])
    await_bytes(c2.at[pl.ds(1, 3)], ssem.at[6])
    await_bytes(r2.at[1], ssem.at[7])
    await_bytes(r2.at[2], ssem.at[8])
    await_bytes(halo, ssem.at[9])
    await_bytes(out_ref.at[core, pl.ds(0, 15)], ssem.at[10])
    await_bytes(out_ref.at[0], ssem.at[11])


def reduce_all(g, c, r):
    vm = pl.BlockSpec(memory_space=VMEM)
    f32 = jnp.float32
    return pl.pallas_call(
        reduce_kernel,
        out_shape=(
            jax.ShapeDtypeStruct((2, 16, 5, 8, 128), f32),
            jax.ShapeDtypeStruct((2, 64), f32),
            jax.ShapeDtypeStruct((8, 64), f32),
        ),
        in_specs=[vm] * 3,
        out_specs=(vm,) * 3,
        scratch_shapes=[
            VMEM((16, 5, 8, 128), f32),
            VMEM((16, 5, 8, 128), f32),
            VMEM((8, 5, 8, 128), f32),
            VMEM((4, 4, 8, 128), f32),
            VMEM((4, 4, 8, 128), f32),
            VMEM((4, 8, 128), f32),
            VMEM((4, 2, 2, 128), f32),
            VMEM((3, 2, 128), f32),
            VMEM((16, 5, 8, 128), f32),
            VMEM((8, 128), f32),
            pltpu.SemaphoreType.DMA((12,)),
            pltpu.SemaphoreType.DMA((12,)),
        ],
        compiler_params=pltpu.CompilerParams(
            collective_id=2, has_side_effects=True, vmem_limit_bytes=40 << 20
        ),
        name="reduce_all",
    )(g, c, r)


FAR = -1e9
F32 = jnp.float32
BF16 = jnp.bfloat16


def times(a, b):
    return jnp.dot(a, b, preferred_element_type=F32)


def times_t(a, b):
    return lax.dot_general(a, b, (((1,), (1,)), ((), ())), preferred_element_type=F32)


def halves(v):
    hi = v.astype(BF16)
    return hi, (v - hi.astype(F32)).astype(BF16)


def turned(v, back):
    n = v.shape[1]
    return pltpu.roll(v, lax.rem(n - back, n), 1)


def lanes(rows, n):
    return lax.broadcasted_iota(jnp.int32, (rows, n), 1)


def block_kernel(
    dil, rowf, colf, rproj, cproj, pw, bias, cw, cot, halo, side,
    out_ref, g_ref, c_ref, r_ref,
    fr, h3, c3, gs, vt, cs,
):
    d1 = dil[0]
    d2 = dil[1]
    r = lax.axis_index("row")
    c = lax.axis_index("col")
    row0 = r * 16
    col0 = c * 256

    fr[...] = jnp.zeros((128, 256), F32)
    for g in range(3):
        for n in range(8):
            fr[g * 16 + 2 * n : g * 16 + 2 * n + 2, :] = rowf[g, n]
    at = row0 - 16 + lax.broadcasted_iota(jnp.int32, (128, 256), 0)
    feat_r = jnp.where((at >= 0) & (at < 512), fr[...], 0.0).astype(BF16)
    wide = colf[...].astype(F32)
    feat_c = jnp.concatenate([wide[:, :8].reshape(288, 128), wide[:, 8:].reshape(288, 128)], axis=1)
    at = col0 - 16 + lax.broadcasted_iota(jnp.int32, (288, 256), 0)
    feat_c = jnp.where((at >= 0) & (at < 2048), feat_c, 0.0)
    feat_c = jnp.concatenate([feat_c, jnp.zeros((96, 256), F32)], axis=0).astype(BF16)
    a_t = times_t(rproj[...].T, feat_r).astype(BF16).astype(F32)
    b_t = times_t(cproj[...].T, feat_c).astype(BF16).astype(F32)

    def taps(v, offset):
        return jnp.concatenate([turned(v, offset + (k - 1) * d1) for k in range(3)], axis=0).astype(BF16)

    pw0 = jnp.concatenate(
        [jnp.concatenate([pw[0, k, q] for q in range(3)], axis=1) for k in range(3)], axis=0
    )
    pw1 = jnp.concatenate(
        [jnp.concatenate([pw[1, k, q] for k in range(3)], axis=1) for q in range(3)], axis=0
    )
    rt = times(pw0.T, taps(a_t, 8)) * 0.5
    ct = times(pw1.T, taps(b_t, 8)) * 0.5
    rt0, rt2 = rt[0:64], rt[128:192]
    rsum = rt0 + rt[64:128] + rt2
    bias_col = jnp.broadcast_to(bias[...] * 0.5, (8, 64)).T[:, 0:1]
    at = col0 - 8 + lanes(64, 384)
    base = ct[64:128] + bias_col + jnp.where((at >= 0) & (at < 2048), 0.0, FAR)
    sums = (base + ct[128:192], base + ct[0:64] + ct[128:192], base + ct[0:64])
    for case in range(3):
        for q in range(3):
            vt[case * 3 + q] = turned(sums[case], 8 + (q - 1) * d2)[:, 0:256]
    near, far = [], []
    for q in range(3):
        at = col0 + (q - 1) * d2 + lanes(1, 256)
        near.append(jnp.where(at - d1 < 0, 1.0, 0.0))
        far.append(jnp.where(at + d1 >= 2048, 1.0, 0.0))

    for e in range(32):
        i = row0 - 8 + e
        case = jnp.where(i - d1 < 0, 0, jnp.where(i + d1 >= 512, 2, 1))
        gate = jnp.where((i >= 0) & (i < 512), 0.0, FAR)
        all_e = rsum[:, e : e + 1] + gate
        rt0_e = rt0[:, e : e + 1]
        rt2_e = rt2[:, e : e + 1]
        for q in range(3):
            h = vt[case * 3 + q] + all_e - near[q] * rt0_e - far[q] * rt2_e
            t = jnp.tanh(h)
            h3[q * 64 : (q + 1) * 64, e * 256 : (e + 1) * 256] = (h + h * t).astype(BF16)
            if q == 1 and 8 <= e < 24:
                gs[:, (e - 8) * 256 : (e - 7) * 256] = 0.5 + 0.5 * t + h * (0.5 - 0.5 * t * t)

    lane = lanes(64, 128)
    for e in range(32):
        if e < 8:
            x0, x1, slot, n = halo[0, e, :, 0:128], halo[0, e, :, 128:256], 0, 8 + e
        elif e < 24:
            x0, x1, slot, n = cot[e - 8, :, 0:128], cot[e - 8, :, 128:256], 1, e - 8
        else:
            x0, x1, slot, n = halo[1, e - 24, :, 0:128], halo[1, e - 24, :, 128:256], 2, e - 24
        i = row0 - 8 + e
        ok = (i >= 0) & (i < 512)
        before = side[0, slot]
        after = side[1, slot]
        if slot != 1:
            keep = jnp.where(ok, 1.0, 0.0).astype(BF16)
            x0, x1 = x0 * keep, x1 * keep
        before = before * jnp.where(ok & (c > 0), 1.0, 0.0).astype(BF16)
        after = after * jnp.where(ok & (c < 7), 1.0, 0.0).astype(BF16)
        cols = slice(e * 256, e * 256 + 128)
        cols1 = slice(e * 256 + 128, e * 256 + 256)
        c3[64:128, cols] = x0
        c3[64:128, cols1] = x1
        r0 = pltpu.roll(x0, d2, 1)
        r1 = pltpu.roll(x1, d2, 1)
        rp = pltpu.roll(before, lax.rem(120 - 8 * n + d2 + 128, 128), 1)
        c3[128:192, cols] = jnp.where(lane < d2, rp, r0)
        c3[128:192, cols1] = jnp.where(lane < d2, r0, r1)
        l0 = pltpu.roll(x0, 128 - d2, 1)
        l1 = pltpu.roll(x1, 128 - d2, 1)
        rn = pltpu.roll(after, lax.rem(256 - 8 * n - d2, 128), 1)
        c3[0:64, cols] = jnp.where(lane >= 128 - d2, l1, l0)
        c3[0:64, cols1] = jnp.where(lane >= 128 - d2, rn, l1)

    wf = [cw[k].reshape(192, 64).T for k in range(3)]
    wb = [jnp.concatenate([cw[k, q] for q in range(3)], axis=1) for k in range(3)]
    live = [1.0 - near[1], None, 1.0 - far[1]]
    rs = [jnp.zeros((64, 128), F32) for _ in range(3)]
    gc = [jnp.zeros((64, 192), F32) for _ in range(3)]
    cs[...] = jnp.zeros((3, 64, 256), F32)
    for n in range(4):
        mixed = jnp.zeros((64, 1024), F32)
        back = jnp.zeros((64, 1024), F32)
        own = h3[64:128, 2048 + n * 1024 : 3072 + n * 1024]
        for k in range(3):
            ahead = pl.multiple_of((8 + (k - 1) * d2) * 256 + n * 1024, 256)
            behind = pl.multiple_of((8 - (k - 1) * d2) * 256 + n * 1024, 256)
            mixed = mixed + times(wf[k], h3[:, pl.ds(ahead, 1024)])
            grads = c3[:, pl.ds(behind, 1024)]
            back = back + times(wb[k], grads)
            gc[k] = gc[k] + times_t(own, grads)
        mixed = (own.astype(F32) + mixed).astype(BF16)
        for m in range(4):
            i = n * 4 + m
            span = slice(m * 256, (m + 1) * 256)
            out_ref[i] = mixed[:, span]
            d = (cot[i].astype(F32) + back[:, span]) * gs[:, i * 256 : (i + 1) * 256]
            cs[1] = cs[1] + d
            cs[0] = cs[0] + d * jnp.where(row0 + i - d1 >= 0, 1.0, 0.0)
            cs[2] = cs[2] + d * jnp.where(row0 + i + d1 < 512, 1.0, 0.0)
            for q in range(3):
                part = d if live[q] is None else d * live[q]
                rs[q] = jnp.where(lane == i, jnp.sum(part, axis=1, keepdims=True), rs[q])

    rs_hi, rs_lo = halves(jnp.concatenate(rs, axis=0))
    cs_all = cs[...].reshape(192, 256)
    cs_hi, cs_lo = halves(cs_all)
    br = times(pw0, rs_hi) + times(pw0, rs_lo)
    bc = times(pw1, cs_hi) + times(pw1, cs_lo)
    bc = jnp.concatenate([bc, jnp.zeros((192, 128), F32)], axis=1)
    dr = sum(pltpu.roll(br[k * 64 : (k + 1) * 64], 16 + (k - 1) * d1, 1) for k in range(3))
    dc = sum(pltpu.roll(bc[q * 64 : (q + 1) * 64], 16 + (q - 1) * d1, 1) for q in range(3))
    at = row0 - 16 + lane
    dr = jnp.where((at >= 0) & (at < 512), dr, 0.0)
    at = col0 - 16 + lanes(64, 384)
    dc = jnp.where((at >= 0) & (at < 2048), dc, 0.0)
    dr_hi, dr_lo = halves(dr)
    dc_hi, dc_lo = halves(dc)
    row_proj_g = (times(dr_hi, feat_r) + times(dr_lo, feat_r)).T
    col_proj_g = (times(dc_hi, feat_c) + times(dc_lo, feat_c)).T
    a_own = taps(a_t, 16)
    b_own = taps(b_t, 16)[:, 0:256]
    p0 = times_t(a_own, rs_hi) + times_t(a_own, rs_lo)
    p1 = times_t(b_own, cs_hi) + times_t(b_own, cs_lo)
    bias_g = jnp.broadcast_to(jnp.sum(cs[1], axis=1, keepdims=True), (64, 64)).T

    blocks = [row_proj_g[n * 64 : (n + 1) * 64] for n in range(4)]
    blocks += [col_proj_g[n * 64 : (n + 1) * 64] for n in range(4)]
    for k in range(3):
        for q in range(3):
            blocks.append(p0[k * 64 : (k + 1) * 64, q * 64 : (q + 1) * 64])
    for k in range(3):
        for q in range(3):
            blocks.append(p1[q * 64 : (q + 1) * 64, k * 64 : (k + 1) * 64])
    for k in range(3):
        for q in range(3):
            blocks.append(gc[k][:, q * 64 : (q + 1) * 64])
    blocks.append(bias_g)
    for b in range(18):
        g_ref[8 * b : 8 * b + 8] = jnp.concatenate([blocks[b], blocks[b + 18]], axis=1).reshape(8, 8, 128)
    g_ref[144:160] = jnp.zeros((16, 8, 128), F32)

    dr_p = dr.T
    dc_p = dc.T
    for n in range(32):
        z_hi, x, core = n // 8, (n // 2) % 4, n % 2
        if n == 0:
            extra = dc_p[272:280]
        elif n == 31:
            extra = dc_p[8:16]
        else:
            extra = jnp.zeros((8, 64), F32)
        c_ref[core * 16 + x * 4 + z_hi] = jnp.concatenate([dc_p[16 + 8 * n : 24 + 8 * n], extra], axis=1)
    for n in range(8):
        h = 32 + 2 * n if n < 4 else 2 * n
        r_ref[n] = jnp.concatenate([dr_p[16 + 2 * n : 18 + 2 * n], dr_p[h : h + 2]], axis=1)


def block(dil, *arrays):
    vm = pl.BlockSpec(memory_space=VMEM)
    return pl.pallas_call(
        block_kernel,
        out_shape=(
            jax.ShapeDtypeStruct((16, 64, 256), BF16),
            jax.ShapeDtypeStruct((160, 8, 128), F32),
            jax.ShapeDtypeStruct((32, 8, 128), F32),
            jax.ShapeDtypeStruct((8, 2, 128), F32),
        ),
        in_specs=[pl.BlockSpec(memory_space=pltpu.SMEM)] + [vm] * len(arrays),
        out_specs=(vm,) * 4,
        scratch_shapes=[
            VMEM((128, 256), F32),
            VMEM((192, 8192), BF16),
            VMEM((192, 8192), BF16),
            VMEM((64, 4096), F32),
            VMEM((9, 64, 256), F32),
            VMEM((3, 64, 256), F32),
        ],
        compiler_params=pltpu.CompilerParams(vmem_limit_bytes=40 << 20),
        name="block",
    )(dil, *arrays)


def shards(
    row_features,
    col_features,
    row_proj,
    col_proj,
    pair_weight,
    pair_bias,
    conv_weight,
    dilations,
    cotangent,
):
    cot_t = jnp.swapaxes(cotangent, 0, 1)
    cf = jnp.concatenate([col_features[:, :128], col_features[:, 128:]], axis=0)
    row_f, col_f, halo, side = gather_all(row_features.astype(F32), cf, cot_t)
    out_t, packed, pieces_c, pieces_r = block(
        dilations, row_f, col_f, row_proj, col_proj, pair_weight,
        pair_bias.reshape(1, 64), conv_weight, cot_t, halo, side,
    )
    total, own_rows, own_cols = reduce_all(
        packed.reshape(2, 16, 5, 8, 128),
        pieces_c.reshape(2, 4, 4, 8, 128),
        pieces_r.reshape(4, 2, 2, 128),
    )
    d_rows = own_rows.astype(BF16)
    d_cols = own_cols.astype(BF16)
    grad_row_features = times(d_rows, row_proj.T)
    grad_col_features = times(d_cols, col_proj.T)
    total = total.reshape(1280, 128)
    low, high = total[:, :64], total[:, 64:]
    pair = jnp.concatenate([low[512:1152], high[0:512]]).reshape(2, 3, 3, 64, 64)
    return (
        jnp.swapaxes(out_t, 0, 1),
        grad_row_features,
        grad_col_features,
        low[0:256],
        low[256:512],
        pair,
        high[1088],
        high[512:1088].reshape(3, 3, 64, 64),
    )


def solution(mesh):
    return jax.shard_map(
        shards,
        mesh=mesh,
        in_specs=(
            P(("row", "col"), None),
            P(("col", "row"), None),
            P(),
            P(),
            P(),
            P(),
            P(),
            P(),
            P(None, "row", "col"),
        ),
        out_specs=(
            P(None, "row", "col"),
            P(("row", "col"), None),
            P(("col", "row"), None),
            P(),
            P(),
            P(),
            P(),
            P(),
        ),
        check_vma=False,
    )
```

time: 128 us -> 75.6 us (0.59)
  matrix products: 37.1 us -> 1.42 us
  between operations: 12.2 us -> 0.76 us
  Pallas kernels: 56.9 us -> 64.7 us
  local copies, waits for them, and re-layouts: 13.7 us -> 6.98 us
  other arithmetic: 7 us -> 1.55 us
    dot_general x43 -> x2, matrix products: 37.1 us -> 1.42 us  [times(): return jnp.dot(a, b, preferred_element_type=F32)]
    pallas_call x1 -> x2, Pallas kernels: 30.1 us -> 37.8 us  [the longest x1 29.6 us: reduce_all(): pl.pallas_call(reduce_kernel, out_shape=(jax.ShapeDtypeStruct((2, 16, 5,...]
    select_n x4 -> x0, other arithmetic: 2.8 us -> none  [the longest x1 2.61 us: shards(): jnp.where(row_inside[None, :, None] * col_inside[None, None, :] > 0, grad...]
    and x10 -> x0, other arithmetic: 2.69 us -> none  [the longest x8 2.67 us: line_valid(): (cells + (tap_idx - 1) * dilation >= 0) & (cells + (tap_idx - 1) * dilati...]
    reshape x8 -> x0, local copies, waits for them, and re-layouts: 2.31 us -> none  [the longest x1 0.98 us: shards(): total[32768:106496].reshape(2, 3, 3, 64, 64)]
    add x4 -> x0, local copies, waits for them, and re-layouts: 1.86 us -> none  [the longest x2 1.51 us: shards(): sum((placed(back_cols[k], margin + (k - 1) * first_rate, cols_here + 2 *...]
    unnamed x38 -> x20, local copies, waits for them, and re-layouts: 5.17 us -> 5.37 us
where the time goes in v2:
time: 75.6 us; the launch traced here: 75.4 us
  Pallas kernels  64.7 us (86%)
  local copies, waits for them, and re-layouts  6.98 us (9%)
  other arithmetic  1.55 us (2%)
  matrix products  1.42 us (2%)
  between operations  0.76 us (1%)
    pallas_call x1, Pallas kernels, reduce_all(): pl.pallas_call(reduce_kernel, out_shape=(jax.ShapeDtypeStruct((2, 16, 5,...  29.6 us
    pallas_call x1, Pallas kernels, gather_all(): pl.pallas_call(gather_kernel, out_shape=(jax.ShapeDtypeStruct((3, 8, 2, 2...  26.9 us
    pallas_call x1, Pallas kernels, block(): pl.pallas_call(block_kernel, out_shape=(jax.ShapeDtypeStruct((16, 64, 256...  8.18 us
    unnamed x20, local copies, waits for them, and re-layouts  5.37 us

profile of v2, /device:TPU:1, one launch (start us, length us, event | category | flops | bytes accessed | tf_op | source)
XLA Modules:
  0.0 75.4 jit_solution(18154680862873142930)
XLA Ops:
  0.6 0.7 convert_element_type.9.rf_ref
  1.3 0.0 copy-done.6
  1.3 0.0 copy-start.5
  1.4 0.9 %copy.18.rproj = bf16[256,64]{1,0:T(8,128)(2,1)S(1)} copy(bf16[256,64]{0,1:T(8,128)(2,1)} %param.11) | data formatting | bytes 65536 | tf_op args[2]
  2.2 0.1 copy.19.cproj
  2.4 1.2 %copy.26 = bf16[64,16,256]{2,0,1:T(8,128)(2,1)S(1)} copy(bf16[64,16,256]{2,1,0:T(8,128)(2,1)} %param.17) | data formatting | bytes 1048576 | tf_op args[8]
  3.6 0.0 copy-start
  3.6 0.0 copy-start.1
  3.6 26.9 %gather_all.1 = (f32[3,8,2,256]{3,2,1,0:T(2,128)S(1)}, bf16[36,16,128]{2,1,0:T(8,128)(2,1)S(1)}, bf16[2,8,64,256]{3,2,1,0:T(8,128)(2,1)S(1)}, bf16[2,3,64,128]{3,2,1,0:T(8,128)(2,1)S(1)}) custom-call(f32[2,256]{1,0:T(2,128)S(1)} %convert_element_type.9.rf_ref, bf16[16,128]{1,0:T(8,128)(2,1)S(1)} %pad_maximum_fusion.1.cf_ref, bf16[16,64,256]{2,1,0:T(8,128)(2,1)S(1)} %bitcast.15), custom_call_target="tpu_custom_call" | custom-call | tf_op jit(solution)/shard_map/gather_all/pallas_call | solution.py:118
  30.5 0.0 copy-start.2
  30.5 0.0 copy-start.3
  30.5 0.6 copy-done.2
  31.1 0.0 copy-done.3
  31.1 8.2 %block.1 = (bf16[16,64,256]{2,1,0:T(8,128)(2,1)S(1)}, f32[160,8,128]{2,1,0:T(8,128)S(1)}, f32[32,8,128]{2,1,0:T(8,128)S(1)}, f32[8,2,128]{2,1,0:T(2,128)S(1)}) custom-call(s32[2]{0:T(128)S(1)} %copy-done.2, f32[3,8,2,256]{3,2,1,0:T(2,128)S(1)} %get-tuple-element.19.rowf, bf16[36,16,128]{2,1,0:T(8,128)(2,1)S(1)} %get-tuple-element.20.colf, ...), custom_call_target="tpu_custom_call" | custom-call | tf_op jit(solution)/shard_map/block/pallas_call | solution.py:487
  39.3 1.1 %copy.22 = bf16[64,16,256]{2,1,0:T(8,128)(2,1)} copy(bf16[64,16,256]{2,0,1:T(8,128)(2,1)S(1)} %bitcast.23) | data formatting | bytes 1048576
  40.4 29.6 %reduce_all.1 = (f32[2,16,5,8,128]{4,3,2,1,0:T(8,128)S(1)}, f32[2,64]{1,0:T(2,128)S(1)}, f32[8,64]{1,0:T(8,128)S(1)}) custom-call(f32[2,16,5,8,128]{4,3,2,1,0:T(8,128)S(1)} %bitcast.22, f32[2,4,4,8,128]{4,3,2,1,0:T(8,128)S(1)} %bitcast.24, f32[4,2,2,128]{3,2,1,0:T(2,128)S(1)} %bitcast.25), custom_call_target="tpu_custom_call" | custom-call | tf_op jit(solution)/shard_map/reduce_all/pallas_call | solution.py:246
  70.1 0.6 slice_bitcast_fusion
  70.6 0.7 fusion.2
  71.3 0.7 fusion
  72.1 0.1 slice.43
  72.2 0.7 copy.24
  72.9 0.7 copy.23
  73.6 0.9 %slice.45 = f32[576,64]{1,0:T(8,128)} slice(f32[1280,128]{1,0:T(8,128)S(1)} %bitcast.20), slice={[512:1088], [64:128]} | slice | bytes 294912 | tf_op jit(solution)/shard_map/slice | solution.py:548
  74.5 0.9 %pad_maximum_fusion = f32[1152,64]{1,0:T(8,128)} fusion(f32[512,64]{1,0:T(8,128)S(1)} %slice.43, f32[640,64]{1,0:T(8,128)S(1)} %slice.42), kind=kLoop, calls=%fused_computation | loop fusion | flops 73728 | bytes 589824 | tf_op jit(solution)/shard_map/concatenate | solution.py:539
  (10 shorter events, 0.1 us)
Async XLA Ops:
  0.6 0.7 copy-start.6
  1.3 0.9 %copy-start.5 = (bf16[256,64]{0,1:T(8,128)(2,1)S(1)}, bf16[256,64]{0,1:T(8,128)(2,1)}, u32[]{:S(2)}) copy-start(bf16[256,64]{0,1:T(8,128)(2,1)} %param.12) | copy-start | bytes 98308
  3.6 26.9 %copy-start = (bf16[2,3,3,64,64]{4,3,2,1,0:T(8,128)(2,1)S(1)}, bf16[2,3,3,64,64]{4,3,2,1,0:T(8,128)(2,1)}, u32[]{:S(2)}) copy-start(bf16[2,3,3,64,64]{4,3,2,1,0:T(8,128)(2,1)} %pw.1) | copy-start | bytes 442372
  3.6 26.9 %copy-start.1 = (bf16[3,3,64,64]{3,2,1,0:T(8,128)(2,1)S(1)}, bf16[3,3,64,64]{3,2,1,0:T(8,128)(2,1)}, u32[]{:S(2)}) copy-start(bf16[3,3,64,64]{3,2,1,0:T(8,128)(2,1)} %cw.1) | copy-start | bytes 221188
  30.5 0.7 copy-start.2
  30.5 0.7 copy-start.3
  40.4 30.2 %copy-start.4 = (bf16[256,64]{0,1:T(8,128)(2,1)S(1)}, bf16[256,64]{0,1:T(8,128)(2,1)}, u32[]{:S(2)}) copy-start(bf16[256,64]{0,1:T(8,128)(2,1)} %param.11) | copy-start | bytes 98308

commit v3 on v2

v3 whole, which is shorter than its diff:
```python
import functools

import jax
import jax.numpy as jnp
from jax import lax
from jax.experimental import pallas as pl
from jax.experimental.pallas import tpu as pltpu
from jax.sharding import PartitionSpec as P

MAX_DILATION = 8
MESH = pl.DeviceIdType.MESH
VMEM = pltpu.VMEM


def places():
    r = lax.axis_index("row")
    c = lax.axis_index("col")
    return r, c, r // 8, lax.rem(r // 2, 4), lax.rem(r, 2), c // 2, lax.rem(c, 2)


def device_at(z_hi, x, core, y, z_lo):
    return ((z_hi * 4 + x) * 2 + core, y * 2 + z_lo)


def signal(barrier, target):
    pl.semaphore_signal(barrier, inc=1, device_id=target, device_id_type=MESH)


def push(src, dst, send_sem, recv_sem, target):
    pltpu.make_async_remote_copy(
        src_ref=src,
        dst_ref=dst,
        send_sem=send_sem,
        recv_sem=recv_sem,
        device_id=target,
        device_id_type=MESH,
    ).start()


def await_bytes(ref, sem):
    pltpu.make_async_copy(ref, ref, sem).wait()


FAR = -1e9
F32 = jnp.float32
BF16 = jnp.bfloat16


def times(a, b):
    return jnp.dot(a, b, preferred_element_type=F32)


def times_t(a, b):
    return lax.dot_general(a, b, (((1,), (1,)), ((), ())), preferred_element_type=F32)


def halves(v):
    hi = v.astype(BF16)
    return hi, (v - hi.astype(F32)).astype(BF16)


def turned(v, back):
    n = v.shape[1]
    return pltpu.roll(v, lax.rem(n - back, n), 1)


def lanes(rows, n):
    return lax.broadcasted_iota(jnp.int32, (rows, n), 1)


def main_kernel(
    dil, rf, cf, rproj, cproj, pw, bias, cw, cot,
    out_ref, sum_ref, drow_ref, dcol_ref,
    rows, cols, halo, side, pack, rf_wide, cf_tall,
    fr, h3, c3, gs, vt, cs,
    g, g0, red, g1, gz, pc, c0, c1, c2, c_halo, pr, r1, r2,
    ssem, rsem, ssem2, rsem2,
):
    d1 = dil[0]
    d2 = dil[1]
    r, c, z_hi, x, core, y, z_lo = places()
    row0 = r * 16
    col0 = c * 256
    up, down = lax.rem(r + 31, 32), lax.rem(r + 1, 32)
    left, right = lax.rem(c + 7, 8), lax.rem(c + 1, 8)
    a = x * 4 + y
    z = z_hi * 2 + z_lo
    sibling = device_at(z_hi, x, 1 - core, y, z_lo)

    def plane(t):
        other = lax.rem(a + t, 16)
        return other, device_at(z_hi, other // 4, core, lax.rem(other, 4), z_lo)

    def along_z(t):
        other = lax.rem(z + t, 8)
        return device_at(other // 2, x, core, y, lax.rem(other, 2))

    barrier = pltpu.get_barrier_semaphore()

    @pl.loop(1, 32)
    def _(t):
        signal(barrier, (lax.rem(r + t, 32), c))

    @pl.loop(1, 8)
    def _(t):
        signal(barrier, (r, lax.rem(c + t, 8)))

    for r_to in (up, down):
        for c_to in (left, right):
            signal(barrier, (r_to, c_to))
    for dx in range(1, 4):
        for dy in range(1, 4):
            signal(barrier, device_at(z_hi, lax.rem(x + dx, 4), core, lax.rem(y + dy, 4), z_lo))
    for dz in range(1, 4):
        signal(barrier, device_at(lax.rem(z_hi + dz, 4), x, core, y, 1 - z_lo))

    own_rf = rf[...].astype(F32)
    rf_wide[...] = own_rf
    rows[1, c] = own_rf
    own_cf = cf[...].astype(F32)
    own_cf = jnp.concatenate([own_cf[:, 0:128], own_cf[:, 128:256]], axis=0).astype(BF16)
    cf_tall[...] = own_cf
    cols[r + 2] = own_cf
    group = lanes(64, 128) // 8
    first = jnp.zeros((64, 128), jnp.float32)
    last = jnp.zeros((64, 128), jnp.float32)
    for i in range(16):
        head = cot[i, :, 0:128].astype(jnp.float32)
        tail = cot[i, :, 128:256].astype(jnp.float32)
        first = jnp.where(group == i, pltpu.roll(head, 8 * i, 1) if i else head, first)
        last = jnp.where(group == i, pltpu.roll(tail, (8 * i + 8) % 128, 1) if i < 15 else tail, last)
    pack[0] = first.astype(jnp.bfloat16)
    pack[1] = last.astype(jnp.bfloat16)
    pl.semaphore_wait(barrier, 31 + 7 + 4 + 9 + 3)

    @pl.loop(1, 32)
    def _(t):
        push(cf_tall, cols.at[r + 2], ssem.at[2], rsem.at[2], (lax.rem(r + t, 32), c))

    @pl.loop(1, 8)
    def _(t):
        push(rf_wide, rows.at[1, c], ssem.at[3], rsem.at[3], (r, lax.rem(c + t, 8)))

    for slot, r_to in ((2, up), (1, r), (0, down)):
        push(pack.at[0], side.at[1, slot], ssem.at[4], rsem.at[4], (r_to, left))
        push(pack.at[1], side.at[0, slot], ssem.at[4], rsem.at[4], (r_to, right))
    push(cot.at[pl.ds(8, 8)], halo.at[0], ssem.at[0], rsem.at[0], (down, c))
    push(cot.at[pl.ds(0, 8)], halo.at[1], ssem.at[1], rsem.at[1], (up, c))

    pw0 = jnp.concatenate(
        [jnp.concatenate([pw[0, k, q] for q in range(3)], axis=1) for k in range(3)], axis=0
    )
    pw1 = jnp.concatenate(
        [jnp.concatenate([pw[1, k, q] for k in range(3)], axis=1) for q in range(3)], axis=0
    )
    wf = [cw[k].reshape(192, 64).T for k in range(3)]
    wb = [jnp.concatenate([cw[k, q] for q in range(3)], axis=1) for k in range(3)]
    lane = lanes(64, 128)

    def taps(v, offset):
        return jnp.concatenate([turned(v, offset + (k - 1) * d1) for k in range(3)], axis=0).astype(BF16)

    def cotangent_row(e):
        if e < 8:
            x0, x1, slot, n = halo[0, e, :, 0:128], halo[0, e, :, 128:256], 0, 8 + e
        elif e < 24:
            x0, x1, slot, n = cot[e - 8, :, 0:128], cot[e - 8, :, 128:256], 1, e - 8
        else:
            x0, x1, slot, n = halo[1, e - 24, :, 0:128], halo[1, e - 24, :, 128:256], 2, e - 24
        i = row0 - 8 + e
        ok = (i >= 0) & (i < 512)
        before = side[0, slot]
        after = side[1, slot]
        if slot != 1:
            keep = jnp.where(ok, 1.0, 0.0).astype(BF16)
            x0, x1 = x0 * keep, x1 * keep
        before = before * jnp.where(ok & (c > 0), 1.0, 0.0).astype(BF16)
        after = after * jnp.where(ok & (c < 7), 1.0, 0.0).astype(BF16)
        low, high = slice(0, 128), slice(128, 256)
        c3[e, 64:128, low] = x0
        c3[e, 64:128, high] = x1
        r0 = pltpu.roll(x0, d2, 1)
        r1 = pltpu.roll(x1, d2, 1)
        rp = pltpu.roll(before, lax.rem(120 - 8 * n + d2 + 128, 128), 1)
        c3[e, 128:192, low] = jnp.where(lane < d2, rp, r0)
        c3[e, 128:192, high] = jnp.where(lane < d2, r0, r1)
        l0 = pltpu.roll(x0, 128 - d2, 1)
        l1 = pltpu.roll(x1, 128 - d2, 1)
        rn = pltpu.roll(after, lax.rem(256 - 8 * n - d2, 128), 1)
        c3[e, 0:64, low] = jnp.where(lane >= 128 - d2, l1, l0)
        c3[e, 0:64, high] = jnp.where(lane >= 128 - d2, rn, l1)

    await_bytes(rows.at[1, pl.ds(0, 7)], rsem.at[3])
    push(rows.at[1], rows.at[0], ssem.at[5], rsem.at[5], (down, c))
    push(rows.at[1], rows.at[2], ssem.at[6], rsem.at[6], (up, c))
    await_bytes(side, rsem.at[4])
    for e in range(8, 24):
        cotangent_row(e)
    await_bytes(cols.at[pl.ds(2, 31)], rsem.at[2])
    push(cols.at[pl.ds(2, 2)], cols.at[pl.ds(34, 2)], ssem.at[7], rsem.at[7], (r, left))
    push(cols.at[pl.ds(32, 2)], cols.at[pl.ds(0, 2)], ssem.at[8], rsem.at[8], (r, right))

    await_bytes(rows.at[0], rsem.at[5])
    await_bytes(rows.at[2], rsem.at[6])
    fr[...] = jnp.zeros((128, 256), F32)
    for m in range(3):
        for n in range(8):
            fr[m * 16 + 2 * n : m * 16 + 2 * n + 2, :] = rows[m, n]
    at = row0 - 16 + lax.broadcasted_iota(jnp.int32, (128, 256), 0)
    feat_r = jnp.where((at >= 0) & (at < 512), fr[...], 0.0).astype(BF16)
    a_t = times_t(rproj[...], feat_r).astype(BF16).astype(F32)
    rt = times(pw0.T, taps(a_t, 8)) * 0.5
    rt0, rt2 = rt[0:64], rt[128:192]
    rsum = rt0 + rt[64:128] + rt2
    bias_col = jnp.broadcast_to(bias[...] * 0.5, (8, 64)).T[:, 0:1]
    await_bytes(cols.at[pl.ds(34, 2)], rsem.at[7])
    await_bytes(cols.at[pl.ds(0, 2)], rsem.at[8])
    wide = cols[...].astype(F32)
    feat_c = jnp.concatenate([wide[:, :8].reshape(288, 128), wide[:, 8:].reshape(288, 128)], axis=1)
    at = col0 - 16 + lax.broadcasted_iota(jnp.int32, (288, 256), 0)
    feat_c = jnp.where((at >= 0) & (at < 2048), feat_c, 0.0)
    feat_c = jnp.concatenate([feat_c, jnp.zeros((96, 256), F32)], axis=0).astype(BF16)
    b_t = times_t(cproj[...], feat_c).astype(BF16).astype(F32)
    ct = times(pw1.T, taps(b_t, 8)) * 0.5
    at = col0 - 8 + lanes(64, 384)
    base = ct[64:128] + bias_col + jnp.where((at >= 0) & (at < 2048), 0.0, FAR)
    sums = (base + ct[128:192], base + ct[0:64] + ct[128:192], base + ct[0:64])
    for case in range(3):
        for q in range(3):
            vt[case * 3 + q] = turned(sums[case], 8 + (q - 1) * d2)[:, 0:256]
    near, far = [], []
    for q in range(3):
        at = col0 + (q - 1) * d2 + lanes(1, 256)
        near.append(jnp.where(at - d1 < 0, 1.0, 0.0))
        far.append(jnp.where(at + d1 >= 2048, 1.0, 0.0))

    for e in range(32):
        i = row0 - 8 + e
        case = jnp.where(i - d1 < 0, 0, jnp.where(i + d1 >= 512, 2, 1))
        gate = jnp.where((i >= 0) & (i < 512), 0.0, FAR)
        all_e = rsum[:, e : e + 1] + gate
        rt0_e = rt0[:, e : e + 1]
        rt2_e = rt2[:, e : e + 1]
        for q in range(3):
            h = vt[case * 3 + q] + all_e - near[q] * rt0_e - far[q] * rt2_e
            t = jnp.tanh(h)
            h3[e, q * 64 : (q + 1) * 64, :] = (h + h * t).astype(BF16)
            if q == 1 and 8 <= e < 24:
                gs[:, (e - 8) * 256 : (e - 7) * 256] = 0.5 + 0.5 * t + h * (0.5 - 0.5 * t * t)

    for i in range(16):
        mixed = h3[8 + i, 64:128, :].astype(F32)
        for k in range(3):
            mixed = mixed + times(wf[k], h3[8 + i + (k - 1) * d2])
        out_ref[i] = mixed.astype(BF16)

    await_bytes(halo.at[0], rsem.at[0])
    await_bytes(halo.at[1], rsem.at[1])
    for e in range(8):
        cotangent_row(e)
        cotangent_row(24 + e)
    live = [1.0 - near[1], None, 1.0 - far[1]]
    rs = [jnp.zeros((64, 128), F32) for _ in range(3)]
    gc = [jnp.zeros((64, 192), F32) for _ in range(3)]
    cs[...] = jnp.zeros((3, 64, 256), F32)
    for i in range(16):
        own = h3[8 + i, 64:128, :]
        d = cot[i].astype(F32)
        for k in range(3):
            grads = c3[8 + i - (k - 1) * d2]
            d = d + times(wb[k], grads)
            gc[k] = gc[k] + times_t(own, grads)
        d = d * gs[:, i * 256 : (i + 1) * 256]
        cs[1] = cs[1] + d
        cs[0] = cs[0] + d * jnp.where(row0 + i - d1 >= 0, 1.0, 0.0)
        cs[2] = cs[2] + d * jnp.where(row0 + i + d1 < 512, 1.0, 0.0)
        for q in range(3):
            part = d if live[q] is None else d * live[q]
            rs[q] = jnp.where(lane == i, jnp.sum(part, axis=1, keepdims=True), rs[q])

    rs_hi, rs_lo = halves(jnp.concatenate(rs, axis=0))
    cs_hi, cs_lo = halves(cs[...].reshape(192, 256))
    br = times(pw0, rs_hi) + times(pw0, rs_lo)
    bc = times(pw1, cs_hi) + times(pw1, cs_lo)
    bc = jnp.concatenate([bc, jnp.zeros((192, 128), F32)], axis=1)
    dr = sum(pltpu.roll(br[k * 64 : (k + 1) * 64], 16 + (k - 1) * d1, 1) for k in range(3))
    dc = sum(pltpu.roll(bc[q * 64 : (q + 1) * 64], 16 + (q - 1) * d1, 1) for q in range(3))
    at = row0 - 16 + lane
    dr = jnp.where((at >= 0) & (at < 512), dr, 0.0)
    at = col0 - 16 + lanes(64, 384)
    dc = jnp.where((at >= 0) & (at < 2048), dc, 0.0)
    dr_hi, dr_lo = halves(dr)
    dc_hi, dc_lo = halves(dc)
    row_proj_g = times(dr_hi, feat_r) + times(dr_lo, feat_r)
    col_proj_g = times(dc_hi, feat_c) + times(dc_lo, feat_c)
    a_own = taps(a_t, 16)
    b_own = taps(b_t, 16)[:, 0:256]
    p0 = times_t(a_own, rs_hi) + times_t(a_own, rs_lo)
    p1 = times_t(b_own, cs_hi) + times_t(b_own, cs_lo)
    bias_g = jnp.broadcast_to(jnp.sum(cs[1], axis=1, keepdims=True), (64, 64)).T

    strips = [p0[k * 64 : (k + 1) * 64] for k in range(3)]
    strips += [p1[q * 64 : (q + 1) * 64] for q in range(3)] + gc
    pairs = [row_proj_g[:, 0:128], row_proj_g[:, 128:256], col_proj_g[:, 0:128], col_proj_g[:, 128:256]]
    pairs += [strip[:, 0:128] for strip in strips]
    rest = [strip[:, 128:192] for strip in strips] + [bias_g]
    pairs += [jnp.concatenate([rest[2 * n], rest[2 * n + 1]], axis=1) for n in range(5)]
    for b in range(18):
        for j in range(4):
            tile = 4 * b + j
            g[tile // 36, (tile // 3) % 12, tile % 3] = pairs[b][16 * j : 16 * j + 16]

    dr_p = dr.T
    dc_p = dc.T
    for n in range(32):
        if n == 0:
            extra = dc_p[272:280]
        elif n == 31:
            extra = dc_p[8:16]
        else:
            extra = jnp.zeros((8, 64), F32)
        pc[n % 2, (n // 2) % 4, n // 8] = jnp.concatenate([dc_p[16 + 8 * n : 24 + 8 * n], extra], axis=1)
    for n in range(8):
        h = 32 + 2 * n if n < 4 else 2 * n
        pr[n // 2, n % 2] = jnp.concatenate([dr_p[16 + 2 * n : 18 + 2 * n], dr_p[h : h + 2]], axis=1)

    row_to = jnp.where(c < 4, down, up)
    col_to = jnp.where(r < 16, right, left)
    push(g.at[1 - core], g0, ssem2.at[0], rsem2.at[0], sibling)
    push(pc.at[1 - core], c0, ssem2.at[1], rsem2.at[1], sibling)
    for t in range(1, 4):
        y_to = lax.rem(y + t, 4)
        push(pr.at[y_to], r1.at[t], ssem2.at[4], rsem2.at[4], device_at(z_hi, x, core, y_to, z_lo))
    await_bytes(g0, rsem2.at[0])
    red[...] = (g[core] + g0[...]).astype(BF16)

    @pl.loop(1, 16)
    def _(t):
        other, target = plane(t)

        @pl.when(other < 12)
        def _():
            push(red.at[other], g1.at[t], ssem2.at[2], rsem2.at[2], target)

    await_bytes(c0, rsem2.at[1])
    c0[...] = c0[...] + pc[core]
    for t in range(1, 4):
        x_to = lax.rem(x + t, 4)
        push(c0.at[x_to], c1.at[t], ssem2.at[3], rsem2.at[3], device_at(z_hi, x_to, core, y, z_lo))
    await_bytes(r1.at[pl.ds(1, 3)], rsem2.at[4])
    r1[0] = pr[y] + r1[1] + r1[2] + r1[3]

    @pl.when(a < 12)
    def _():
        await_bytes(g1.at[pl.ds(1, 15)], rsem2.at[2])
        mine = g[core, a] + g0[a]
        for t in range(1, 16):
            mine = mine + g1[t].astype(F32)
        gz[z] = mine.astype(BF16)

        @pl.loop(1, 8)
        def _(t):
            push(gz.at[z], gz.at[z], ssem2.at[5], rsem2.at[5], along_z(t))

    await_bytes(c1.at[pl.ds(1, 3)], rsem2.at[3])
    c1[0] = c0[x] + c1[1] + c1[2] + c1[3]
    for t in range(1, 4):
        z_to = lax.rem(z_hi + t, 4)
        push(c1.at[0, z_to], c2.at[t], ssem2.at[6], rsem2.at[6], device_at(z_to, x, core, y, z_lo))
    push(r1.at[0, 1 - z_lo], r2.at[1], ssem2.at[7], rsem2.at[7], device_at(z_hi, x, core, y, 1 - z_lo))

    @pl.when(a < 12)
    def _():
        await_bytes(gz.at[pl.ds(0, 7)], rsem2.at[5])
        whole = gz[0].astype(F32)
        for t in range(1, 8):
            whole = whole + gz[t].astype(F32)
        sum_ref[core, a] = whole.astype(BF16)

        @pl.loop(1, 16)
        def _(t):
            push(sum_ref.at[core, a], sum_ref.at[core, a], ssem2.at[10], rsem2.at[10], plane(t)[1])

    await_bytes(c2.at[pl.ds(1, 3)], rsem2.at[6])
    await_bytes(r2.at[1], rsem2.at[7])
    c2[0] = c1[0, z_hi] + c2[1] + c2[2] + c2[3]
    r2[0] = r1[0, z_lo] + r2[1]
    push(r2.at[0], r2.at[2], ssem2.at[8], rsem2.at[8], (row_to, c))
    push(c2.at[0], c_halo, ssem2.at[9], rsem2.at[9], (r, col_to))
    await_bytes(r2.at[2], rsem2.at[8])
    await_bytes(c_halo, rsem2.at[9])
    drow_ref[...] = r2[0, :, 0:64] + r2[2, :, 64:128]
    dcol_ref[...] = c2[0, :, 0:64] + c_halo[:, 64:128]

    @pl.when(a < 12)
    def _():
        await_bytes(sum_ref.at[core, pl.ds(0, 11)], rsem2.at[10])

    @pl.when(a >= 12)
    def _():
        await_bytes(sum_ref.at[core], rsem2.at[10])

    push(sum_ref.at[core], sum_ref.at[core], ssem2.at[11], rsem2.at[11], sibling)
    await_bytes(sum_ref.at[0], rsem2.at[11])

    await_bytes(halo.at[0], ssem.at[0])
    await_bytes(halo.at[1], ssem.at[1])
    await_bytes(cols.at[pl.ds(2, 31)], ssem.at[2])
    await_bytes(rows.at[1, pl.ds(0, 7)], ssem.at[3])
    await_bytes(side, ssem.at[4])
    await_bytes(rows.at[0], ssem.at[5])
    await_bytes(rows.at[2], ssem.at[6])
    await_bytes(cols.at[pl.ds(34, 2)], ssem.at[7])
    await_bytes(cols.at[pl.ds(0, 2)], ssem.at[8])
    await_bytes(g0, ssem2.at[0])
    await_bytes(c0, ssem2.at[1])
    await_bytes(c1.at[pl.ds(1, 3)], ssem2.at[3])
    await_bytes(r1.at[pl.ds(1, 3)], ssem2.at[4])
    await_bytes(c2.at[pl.ds(1, 3)], ssem2.at[6])
    await_bytes(r2.at[1], ssem2.at[7])
    await_bytes(r2.at[2], ssem2.at[8])
    await_bytes(c_halo, ssem2.at[9])
    await_bytes(sum_ref.at[0], ssem2.at[11])

    @pl.when(a < 12)
    def _():
        await_bytes(g1.at[pl.ds(0, 11)], ssem2.at[2])
        await_bytes(gz.at[pl.ds(0, 7)], ssem2.at[5])
        await_bytes(g1.at[pl.ds(1, 15)], ssem2.at[10])

    @pl.when(a >= 12)
    def _():
        await_bytes(g1.at[pl.ds(0, 12)], ssem2.at[2])


def main(dil, *arrays):
    vm = pl.BlockSpec(memory_space=VMEM)
    return pl.pallas_call(
        main_kernel,
        out_shape=(
            jax.ShapeDtypeStruct((16, 64, 256), BF16),
            jax.ShapeDtypeStruct((2, 12, 3, 16, 128), BF16),
            jax.ShapeDtypeStruct((2, 64), F32),
            jax.ShapeDtypeStruct((8, 64), F32),
        ),
        in_specs=[pl.BlockSpec(memory_space=pltpu.SMEM)] + [vm] * len(arrays),
        out_specs=(vm,) * 4,
        scratch_shapes=[
            VMEM((3, 8, 2, 256), F32),
            VMEM((36, 16, 128), BF16),
            VMEM((2, 8, 64, 256), BF16),
            VMEM((2, 3, 64, 128), BF16),
            VMEM((2, 64, 128), BF16),
            VMEM((2, 256), F32),
            VMEM((16, 128), BF16),
            VMEM((128, 256), F32),
            VMEM((32, 192, 256), BF16),
            VMEM((32, 192, 256), BF16),
            VMEM((64, 4096), F32),
            VMEM((9, 64, 256), F32),
            VMEM((3, 64, 256), F32),
            VMEM((2, 12, 3, 16, 128), F32),
            VMEM((12, 3, 16, 128), F32),
            VMEM((12, 3, 16, 128), BF16),
            VMEM((16, 3, 16, 128), BF16),
            VMEM((8, 3, 16, 128), BF16),
            VMEM((2, 4, 4, 8, 128), F32),
            VMEM((4, 4, 8, 128), F32),
            VMEM((4, 4, 8, 128), F32),
            VMEM((4, 8, 128), F32),
            VMEM((8, 128), F32),
            VMEM((4, 2, 2, 128), F32),
            VMEM((4, 2, 2, 128), F32),
            VMEM((3, 2, 128), F32),
            pltpu.SemaphoreType.DMA((9,)),
            pltpu.SemaphoreType.DMA((9,)),
            pltpu.SemaphoreType.DMA((12,)),
            pltpu.SemaphoreType.DMA((12,)),
        ],
        compiler_params=pltpu.CompilerParams(
            collective_id=1, has_side_effects=True, vmem_limit_bytes=48 << 20
        ),
        name="main",
    )(dil, *arrays)


def finish_kernel(sums, drow, dcol, rproj, cproj, rp_ref, cp_ref, pair_ref, conv_ref, bias_ref, rf_ref, cf_ref):
    def pair_at(b):
        parts = []
        for j in range(4):
            tile = 4 * b + j
            parts.append(sums[tile // 36, (tile // 3) % 12, tile % 3].astype(F32))
        return jnp.concatenate(parts, axis=0)

    rp_ref[:, 0:128] = pair_at(0)
    rp_ref[:, 128:256] = pair_at(1)
    cp_ref[:, 0:128] = pair_at(2)
    cp_ref[:, 128:256] = pair_at(3)
    strips = [pair_at(4 + n) for n in range(9)]
    rest = []
    for n in range(5):
        both = pair_at(13 + n)
        rest += [both[:, 0:64], both[:, 64:128]]
    for k in range(3):
        for q in range(3):
            near = slice(q * 64, q * 64 + 64)
            pair_ref[k * 3 + q] = strips[k][:, near] if q < 2 else rest[k]
            pair_ref[9 + q * 3 + k] = strips[3 + k][:, near] if q < 2 else rest[3 + k]
            conv_ref[k * 3 + q] = strips[6 + k][:, near] if q < 2 else rest[6 + k]
    bias_ref[...] = rest[9][0:1]
    rf_ref[...] = times(drow[...].astype(BF16), rproj[...])
    cf_ref[...] = times(dcol[...].astype(BF16), cproj[...])


def finish(*arrays):
    vm = pl.BlockSpec(memory_space=VMEM)
    shapes = ((64, 256), (64, 256), (18, 64, 64), (9, 64, 64), (1, 64), (2, 256), (8, 256))
    return pl.pallas_call(
        finish_kernel,
        out_shape=tuple(jax.ShapeDtypeStruct(s, F32) for s in shapes),
        in_specs=[vm] * len(arrays),
        out_specs=(vm,) * len(shapes),
        compiler_params=pltpu.CompilerParams(vmem_limit_bytes=24 << 20),
        name="finish",
    )(*arrays)


def shards(
    row_features,
    col_features,
    row_proj,
    col_proj,
    pair_weight,
    pair_bias,
    conv_weight,
    dilations,
    cotangent,
):
    cot_t = jnp.swapaxes(cotangent, 0, 1)
    row_w, col_w = row_proj.T, col_proj.T
    out_t, sums, own_rows, own_cols = main(
        dilations, row_features, col_features, row_w, col_w, pair_weight,
        pair_bias.reshape(1, 64), conv_weight, cot_t,
    )
    row_g, col_g, pair, conv, bias, row_f, col_f = finish(sums, own_rows, own_cols, row_w, col_w)
    return (
        jnp.swapaxes(out_t, 0, 1),
        row_f,
        col_f,
        row_g.T,
        col_g.T,
        pair.reshape(2, 3, 3, 64, 64),
        bias.reshape(64),
        conv.reshape(3, 3, 64, 64),
    )


def solution(mesh):
    return jax.shard_map(
        shards,
        mesh=mesh,
        in_specs=(
            P(("row", "col"), None),
            P(("col", "row"), None),
            P(),
            P(),
            P(),
            P(),
            P(),
            P(),
            P(None, "row", "col"),
        ),
        out_specs=(
            P(None, "row", "col"),
            P(("row", "col"), None),
            P(("col", "row"), None),
            P(),
            P(),
            P(),
            P(),
            P(),
        ),
        check_vma=False,
    )
```

time: 75.6 us -> 61.5 us (0.81)
  Pallas kernels: 64.7 us -> 57.6 us
  local copies, waits for them, and re-layouts: 6.98 us -> 2.96 us
  other arithmetic: 1.55 us -> 0 us
  matrix products: 1.42 us -> 0 us
    pallas_call x3 -> x2, Pallas kernels: 64.7 us -> 57.6 us  [the longest x1 56.6 us: main(): pl.pallas_call(main_kernel, out_shape=(jax.ShapeDtypeStruct((16, 64, 256)...]
    unnamed x20 -> x18, local copies, waits for them, and re-layouts: 5.37 us -> 2.96 us
    dot_general x2 -> x0, matrix products: 1.42 us -> none  [times(): return jnp.dot(a, b, preferred_element_type=F32)]
    slice x5 -> x0, local copies, waits for them, and re-layouts: 1.02 us -> none  [the longest x1 0.86 us: shards(): high[512:1088].reshape(3, 3, 64, 64)]
    concatenate x2 -> x0, other arithmetic: 0.86 us -> none  [the longest x1 0.86 us: shards(): jnp.concatenate([low[512:1152], high[0:512]]).reshape(2, 3, 3, 64, 64)]
where the time goes in v3:
time: 61.5 us; the launch traced here: 61.3 us
  Pallas kernels  57.6 us (94%)
  local copies, waits for them, and re-layouts  2.96 us (5%)
  between operations  0.76 us (1%)
    pallas_call x1, Pallas kernels, main(): pl.pallas_call(main_kernel, out_shape=(jax.ShapeDtypeStruct((16, 64, 256)...  56.6 us
    unnamed x18, local copies, waits for them, and re-layouts  2.96 us

profile of v3, /device:TPU:1, one launch (start us, length us, event | category | flops | bytes accessed | tf_op | source)
XLA Modules:
  0.0 61.3 jit_solution(7213700932464469032)
XLA Ops:
  0.6 0.0 copy-start
  0.6 0.0 copy-start.1
  0.7 0.0 copy-start.2
  0.7 0.0 copy-start.3
  0.7 0.0 copy-start.4
  0.7 0.0 copy-start.7
  0.7 1.2 %copy.20 = bf16[64,16,256]{2,0,1:T(8,128)(2,1)S(1)} copy(bf16[64,16,256]{2,1,0:T(8,128)(2,1)} %param.17) | data formatting | bytes 1048576 | tf_op args[8]
  1.9 0.0 copy-start.5
  2.0 0.0 copy-start.6
  2.0 0.0 copy-done
  2.0 0.0 copy-done.1
  2.0 0.0 copy-done.2
  2.0 0.0 copy-done.3
  2.0 0.0 copy-done.4
  2.0 0.0 copy-done.7
  2.0 0.6 copy-done.5
  2.6 0.0 copy-done.6
  2.6 56.6 %main.1 = (bf16[16,64,256]{2,1,0:T(8,128)(2,1)S(1)}, bf16[2,12,3,16,128]{4,3,2,1,0:T(8,128)(2,1)S(1)}, f32[2,64]{1,0:T(2,128)S(1)}, f32[8,64]{1,0:T(8,128)S(1)}) custom-call(s32[2]{0:T(128)S(1)} %copy-done.6, bf16[2,256]{1,0:T(2,128)(2,1)S(1)} %copy-done.5, bf16[8,256]{1,0:T(8,128)(2,1)S(1)} %copy-done.4, bf16[64,256]{1,0:T(8,128)(2,1)S(1)} %bitcast.14, ...), custom_call_target="tpu_custom_call" | custom-call | tf_op jit(solution)/shard_map/main/pallas_call | solution.py:438
  59.2 1.1 %copy.18 = bf16[64,16,256]{2,1,0:T(8,128)(2,1)} copy(bf16[64,16,256]{2,0,1:T(8,128)(2,1)S(1)} %bitcast.13) | data formatting | bytes 1048576
  60.3 1.0 %finish.1 = (f32[64,256]{1,0:T(8,128)}, f32[64,256]{1,0:T(8,128)}, f32[18,64,64]{2,1,0:T(8,128)}, f32[9,64,64]{2,1,0:T(8,128)}, f32[1,64]{1,0:T(1,128)}, /*index=5*/f32[2,256]{1,0:T(2,128)}, f32[8,256]{1,0:T(8,128)}) custom-call(bf16[2,12,3,16,128]{4,3,2,1,0:T(8,128)(2,1)S(1)} %get-tuple-element.20.sums, f32[2,64]{1,0:T(2,128)S(1)} %get-tuple-element.21.drow, ...), custom_call_target="tpu_custom_call" | custom-call | tf_op jit(solution)/shard_map/finish/pallas_call | solution.py:518
Async XLA Ops:
  0.6 1.3 %copy-start = (bf16[2,3,3,64,64]{4,3,2,1,0:T(8,128)(2,1)S(1)}, bf16[2,3,3,64,64]{4,3,2,1,0:T(8,128)(2,1)}, u32[]{:S(2)}) copy-start(bf16[2,3,3,64,64]{4,3,2,1,0:T(8,128)(2,1)} %pw.1) | copy-start | bytes 442372
  0.6 1.3 %copy-start.1 = (bf16[3,3,64,64]{3,2,1,0:T(8,128)(2,1)S(1)}, bf16[3,3,64,64]{3,2,1,0:T(8,128)(2,1)}, u32[]{:S(2)}) copy-start(bf16[3,3,64,64]{3,2,1,0:T(8,128)(2,1)} %cw.1) | copy-start | bytes 221188
  0.7 1.3 %copy-start.2 = (bf16[256,64]{0,1:T(8,128)(2,1)S(1)}, bf16[256,64]{0,1:T(8,128)(2,1)}, u32[]{:S(2)}) copy-start(bf16[256,64]{0,1:T(8,128)(2,1)} %param.11) | copy-start | bytes 98308
  0.7 1.3 %copy-start.3 = (bf16[256,64]{0,1:T(8,128)(2,1)S(1)}, bf16[256,64]{0,1:T(8,128)(2,1)}, u32[]{:S(2)}) copy-start(bf16[256,64]{0,1:T(8,128)(2,1)} %param.12) | copy-start | bytes 98308
  0.7 1.3 %copy-start.4 = (bf16[8,256]{1,0:T(8,128)(2,1)S(1)}, bf16[8,256]{1,0:T(8,128)(2,1)}, u32[]{:S(2)}) copy-start(bf16[8,256]{1,0:T(8,128)(2,1)} %cf.1) | copy-start | bytes 12292
  0.7 1.3 %copy-start.7 = (f32[64]{0:T(128)S(1)}, f32[64]{0:T(128)}, u32[]{:S(2)}) copy-start(f32[64]{0:T(128)} %param.14) | copy-start | bytes 772
  1.9 0.7 %copy-start.5 = (bf16[2,256]{1,0:T(2,128)(2,1)S(1)}, bf16[2,256]{1,0:T(2,128)(2,1)}, u32[]{:S(2)}) copy-start(bf16[2,256]{1,0:T(2,128)(2,1)} %rf.1) | copy-start | bytes 3076
  2.0 0.7 %copy-start.6 = (s32[2]{0:T(128)S(1)}, s32[2]{0:T(128)}, u32[]{:S(2)}) copy-start(s32[2]{0:T(128)} %dil.1) | copy-start | bytes 28

commit v4 on v3

--- a/solution.py
+++ b/solution.py
@@ -72,7 +72,7 @@
     dil, rf, cf, rproj, cproj, pw, bias, cw, cot,
     out_ref, sum_ref, drow_ref, dcol_ref,
     rows, cols, halo, side, pack, rf_wide, cf_tall,
-    fr, h3, c3, gs, vt, cs,
+    fr, h3, c3, gs, vt, st, cs,
     g, g0, red, g1, gz, pc, c0, c1, c2, c_halo, pr, r1, r2,
     ssem, rsem, ssem2, rsem2,
 ):
@@ -226,33 +226,30 @@
     base = ct[64:128] + bias_col + jnp.where((at >= 0) & (at < 2048), 0.0, FAR)
     sums = (base + ct[128:192], base + ct[0:64] + ct[128:192], base + ct[0:64])
     for case in range(3):
-        for q in range(3):
-            vt[case * 3 + q] = turned(sums[case], 8 + (q - 1) * d2)[:, 0:256]
+        st[case] = sums[case]
+        vt[case * 3 + 1] = turned(sums[case], 8)[:, 0:256]
     near, far = [], []
     for q in range(3):
         at = col0 + (q - 1) * d2 + lanes(1, 256)
         near.append(jnp.where(at - d1 < 0, 1.0, 0.0))
         far.append(jnp.where(at + d1 >= 2048, 1.0, 0.0))
 
-    for e in range(32):
+    def hidden_row(e, taps_here):
         i = row0 - 8 + e
         case = jnp.where(i - d1 < 0, 0, jnp.where(i + d1 >= 512, 2, 1))
         gate = jnp.where((i >= 0) & (i < 512), 0.0, FAR)
         all_e = rsum[:, e : e + 1] + gate
         rt0_e = rt0[:, e : e + 1]
         rt2_e = rt2[:, e : e + 1]
-        for q in range(3):
+        for q in taps_here:
             h = vt[case * 3 + q] + all_e - near[q] * rt0_e - far[q] * rt2_e
             t = jnp.tanh(h)
             h3[e, q * 64 : (q + 1) * 64, :] = (h + h * t).astype(BF16)
             if q == 1 and 8 <= e < 24:
                 gs[:, (e - 8) * 256 : (e - 7) * 256] = 0.5 + 0.5 * t + h * (0.5 - 0.5 * t * t)
 
-    for i in range(16):
-        mixed = h3[8 + i, 64:128, :].astype(F32)
-        for k in range(3):
-            mixed = mixed + times(wf[k], h3[8 + i + (k - 1) * d2])
-        out_ref[i] = mixed.astype(BF16)
+    for e in range(8, 24):
+        hidden_row(e, (1,))
 
     await_bytes(halo.at[0], rsem.at[0])
     await_bytes(halo.at[1], rsem.at[1])
@@ -347,6 +344,12 @@
     for t in range(1, 4):
         x_to = lax.rem(x + t, 4)
         push(c0.at[x_to], c1.at[t], ssem2.at[3], rsem2.at[3], device_at(z_hi, x_to, core, y, z_lo))
+    for case in range(3):
+        for q in (0, 2):
+            vt[case * 3 + q] = turned(st[case], 8 + (q - 1) * d2)[:, 0:256]
+    for e in range(32):
+        hidden_row(e, (0, 2) if 8 <= e < 24 else (0, 1, 2))
+
     await_bytes(r1.at[pl.ds(1, 3)], rsem2.at[4])
     r1[0] = pr[y] + r1[1] + r1[2] + r1[3]
 
@@ -368,6 +371,12 @@
         z_to = lax.rem(z_hi + t, 4)
         push(c1.at[0, z_to], c2.at[t], ssem2.at[6], rsem2.at[6], device_at(z_to, x, core, y, z_lo))
     push(r1.at[0, 1 - z_lo], r2.at[1], ssem2.at[7], rsem2.at[7], device_at(z_hi, x, core, y, 1 - z_lo))
+
+    for i in range(16):
+        mixed = h3[8 + i, 64:128, :].astype(F32)
+        for k in range(3):
+            mixed = mixed + times(wf[k], h3[8 + i + (k - 1) * d2])
+        out_ref[i] = mixed.astype(BF16)
 
     @pl.when(a < 12)
     def _():
@@ -458,6 +467,7 @@
             VMEM((32, 192, 256), BF16),
             VMEM((64, 4096), F32),
             VMEM((9, 64, 256), F32),
+            VMEM((3, 64, 384), F32),
             VMEM((3, 64, 256), F32),
             VMEM((2, 12, 3, 16, 128), F32),
             VMEM((12, 3, 16, 128), F32),

time: 61.5 us -> 58.6 us (0.953)
  Pallas kernels: 57.6 us -> 54.8 us
    pallas_call x1, Pallas kernels: 56.6 us -> 53.7 us  [main(): pl.pallas_call(main_kernel, out_shape=(jax.ShapeDtypeStruct((16, 64, 256)...]
where the time goes in v4:
time: 58.6 us; the launch traced here: 58.5 us
  Pallas kernels  54.8 us (94%)
  local copies, waits for them, and re-layouts  2.96 us (5%)
  between operations  0.76 us (1%)
    pallas_call x1, Pallas kernels, main(): pl.pallas_call(main_kernel, out_shape=(jax.ShapeDtypeStruct((16, 64, 256)...  53.7 us
    unnamed x18, local copies, waits for them, and re-layouts  2.96 us

profile of v4, /device:TPU:1, one launch (start us, length us, event | category | flops | bytes accessed | tf_op | source)
XLA Modules:
  0.0 58.5 jit_solution(17573140228918679036)
XLA Ops:
  0.6 0.0 copy-start
  0.6 0.0 copy-start.1
  0.7 0.0 copy-start.2
  0.7 0.0 copy-start.3
  0.7 0.0 copy-start.4
  0.7 0.0 copy-start.7
  0.7 1.2 %copy.20 = bf16[64,16,256]{2,0,1:T(8,128)(2,1)S(1)} copy(bf16[64,16,256]{2,1,0:T(8,128)(2,1)} %param.17) | data formatting | bytes 1048576 | tf_op args[8]
  1.9 0.0 copy-start.5
  2.0 0.0 copy-start.6
  2.0 0.0 copy-done
  2.0 0.0 copy-done.1
  2.0 0.0 copy-done.2
  2.0 0.0 copy-done.3
  2.0 0.0 copy-done.4
  2.0 0.0 copy-done.7
  2.0 0.6 %copy-done.5 = bf16[2,256]{1,0:T(2,128)(2,1)S(1)} copy-done((bf16[2,256]{1,0:T(2,128)(2,1)S(1)}, bf16[2,256]{1,0:T(2,128)(2,1)}, u32[]{:S(2)}) %copy-start.5) | copy-done | bytes 1048
  2.6 0.0 copy-done.6
  2.6 53.7 %main.1 = (bf16[16,64,256]{2,1,0:T(8,128)(2,1)S(1)}, bf16[2,12,3,16,128]{4,3,2,1,0:T(8,128)(2,1)S(1)}, f32[2,64]{1,0:T(2,128)S(1)}, f32[8,64]{1,0:T(8,128)S(1)}) custom-call(s32[2]{0:T(128)S(1)} %copy-done.6, bf16[2,256]{1,0:T(2,128)(2,1)S(1)} %copy-done.5, bf16[8,256]{1,0:T(8,128)(2,1)S(1)} %copy-done.4, bf16[64,256]{1,0:T(8,128)(2,1)S(1)} %bitcast.14, ...), custom_call_target="tpu_custom_call" | custom-call | tf_op jit(solution)/shard_map/main/pallas_call | solution.py:447
  56.3 1.1 %copy.18 = bf16[64,16,256]{2,1,0:T(8,128)(2,1)} copy(bf16[64,16,256]{2,0,1:T(8,128)(2,1)S(1)} %bitcast.13) | data formatting | bytes 1048576
  57.4 1.0 %finish.1 = (f32[64,256]{1,0:T(8,128)}, f32[64,256]{1,0:T(8,128)}, f32[18,64,64]{2,1,0:T(8,128)}, f32[9,64,64]{2,1,0:T(8,128)}, f32[1,64]{1,0:T(1,128)}, /*index=5*/f32[2,256]{1,0:T(2,128)}, f32[8,256]{1,0:T(8,128)}) custom-call(bf16[2,12,3,16,128]{4,3,2,1,0:T(8,128)(2,1)S(1)} %get-tuple-element.20.sums, f32[2,64]{1,0:T(2,128)S(1)} %get-tuple-element.21.drow, ...), custom_call_target="tpu_custom_call" | custom-call | tf_op jit(solution)/shard_map/finish/pallas_call | solution.py:528
Async XLA Ops:
  0.6 1.3 %copy-start = (bf16[2,3,3,64,64]{4,3,2,1,0:T(8,128)(2,1)S(1)}, bf16[2,3,3,64,64]{4,3,2,1,0:T(8,128)(2,1)}, u32[]{:S(2)}) copy-start(bf16[2,3,3,64,64]{4,3,2,1,0:T(8,128)(2,1)} %pw.1) | copy-start | bytes 442372
  0.6 1.3 %copy-start.1 = (bf16[3,3,64,64]{3,2,1,0:T(8,128)(2,1)S(1)}, bf16[3,3,64,64]{3,2,1,0:T(8,128)(2,1)}, u32[]{:S(2)}) copy-start(bf16[3,3,64,64]{3,2,1,0:T(8,128)(2,1)} %cw.1) | copy-start | bytes 221188
  0.7 1.3 %copy-start.2 = (bf16[256,64]{0,1:T(8,128)(2,1)S(1)}, bf16[256,64]{0,1:T(8,128)(2,1)}, u32[]{:S(2)}) copy-start(bf16[256,64]{0,1:T(8,128)(2,1)} %param.11) | copy-start | bytes 98308
  0.7 1.3 %copy-start.3 = (bf16[256,64]{0,1:T(8,128)(2,1)S(1)}, bf16[256,64]{0,1:T(8,128)(2,1)}, u32[]{:S(2)}) copy-start(bf16[256,64]{0,1:T(8,128)(2,1)} %param.12) | copy-start | bytes 98308
  0.7 1.3 %copy-start.4 = (bf16[8,256]{1,0:T(8,128)(2,1)S(1)}, bf16[8,256]{1,0:T(8,128)(2,1)}, u32[]{:S(2)}) copy-start(bf16[8,256]{1,0:T(8,128)(2,1)} %cf.1) | copy-start | bytes 12292
  0.7 1.3 %copy-start.7 = (f32[64]{0:T(128)S(1)}, f32[64]{0:T(128)}, u32[]{:S(2)}) copy-start(f32[64]{0:T(128)} %param.14) | copy-start | bytes 772
  1.9 0.7 %copy-start.5 = (bf16[2,256]{1,0:T(2,128)(2,1)S(1)}, bf16[2,256]{1,0:T(2,128)(2,1)}, u32[]{:S(2)}) copy-start(bf16[2,256]{1,0:T(2,128)(2,1)} %rf.1) | copy-start | bytes 3076
  2.0 0.7 %copy-start.6 = (s32[2]{0:T(128)S(1)}, s32[2]{0:T(128)}, u32[]{:S(2)}) copy-start(s32[2]{0:T(128)} %dil.1) | copy-start | bytes 28

commit v5 on v4

--- a/solution.py
+++ b/solution.py
@@ -72,7 +72,7 @@
     dil, rf, cf, rproj, cproj, pw, bias, cw, cot,
     out_ref, sum_ref, drow_ref, dcol_ref,
     rows, cols, halo, side, pack, rf_wide, cf_tall,
-    fr, h3, c3, gs, vt, st, cs,
+    mix, fr, h3, c3, gs, vt, st, cs,
     g, g0, red, g1, gz, pc, c0, c1, c2, c_halo, pr, r1, r2,
     ssem, rsem, ssem2, rsem2,
 ):
@@ -97,9 +97,9 @@
 
     barrier = pltpu.get_barrier_semaphore()
 
-    @pl.loop(1, 32)
+    @pl.loop(12, 43)
     def _(t):
-        signal(barrier, (lax.rem(r + t, 32), c))
+        signal(barrier, (lax.rem(r + t + t // 32, 32), c))
 
     @pl.loop(1, 8)
     def _(t):
@@ -121,6 +121,16 @@
     own_cf = jnp.concatenate([own_cf[:, 0:128], own_cf[:, 128:256]], axis=0).astype(BF16)
     cf_tall[...] = own_cf
     cols[r + 2] = own_cf
+    pl.semaphore_wait(barrier, 31 + 7 + 4 + 9 + 3)
+
+    @pl.loop(12, 43)
+    def _(t):
+        push(cf_tall, cols.at[r + 2], ssem.at[2], rsem.at[2], (lax.rem(r + t + t // 32, 32), c))
+
+    @pl.loop(1, 8)
+    def _(t):
+        push(rf_wide, rows.at[1, c], ssem.at[3], rsem.at[3], (r, lax.rem(c + t, 8)))
+
     group = lanes(64, 128) // 8
     first = jnp.zeros((64, 128), jnp.float32)
     last = jnp.zeros((64, 128), jnp.float32)
@@ -131,16 +141,6 @@
         last = jnp.where(group == i, pltpu.roll(tail, (8 * i + 8) % 128, 1) if i < 15 else tail, last)
     pack[0] = first.astype(jnp.bfloat16)
     pack[1] = last.astype(jnp.bfloat16)
-    pl.semaphore_wait(barrier, 31 + 7 + 4 + 9 + 3)
-
-    @pl.loop(1, 32)
-    def _(t):
-        push(cf_tall, cols.at[r + 2], ssem.at[2], rsem.at[2], (lax.rem(r + t, 32), c))
-
-    @pl.loop(1, 8)
-    def _(t):
-        push(rf_wide, rows.at[1, c], ssem.at[3], rsem.at[3], (r, lax.rem(c + t, 8)))
-
     for slot, r_to in ((2, up), (1, r), (0, down)):
         push(pack.at[0], side.at[1, slot], ssem.at[4], rsem.at[4], (r_to, left))
         push(pack.at[1], side.at[0, slot], ssem.at[4], rsem.at[4], (r_to, right))
@@ -331,8 +331,9 @@
     await_bytes(g0, rsem2.at[0])
     red[...] = (g[core] + g0[...]).astype(BF16)
 
-    @pl.loop(1, 16)
-    def _(t):
+    @pl.loop(6, 21)
+    def _(u):
+        t = lax.rem(u + u // 16, 16)
         other, target = plane(t)
 
         @pl.when(other < 12)
@@ -361,8 +362,9 @@
             mine = mine + g1[t].astype(F32)
         gz[z] = mine.astype(BF16)
 
-        @pl.loop(1, 8)
-        def _(t):
+        @pl.loop(3, 10)
+        def _(u):
+            t = lax.rem(u + u // 8, 8)
             push(gz.at[z], gz.at[z], ssem2.at[5], rsem2.at[5], along_z(t))
 
     await_bytes(c1.at[pl.ds(1, 3)], rsem2.at[3])
@@ -376,7 +378,8 @@
         mixed = h3[8 + i, 64:128, :].astype(F32)
         for k in range(3):
             mixed = mixed + times(wf[k], h3[8 + i + (k - 1) * d2])
-        out_ref[i] = mixed.astype(BF16)
+        mix[i] = mixed.astype(BF16)
+    out_ref[...] = jnp.swapaxes(mix[...], 0, 1)
 
     @pl.when(a < 12)
     def _():
@@ -386,8 +389,9 @@
             whole = whole + gz[t].astype(F32)
         sum_ref[core, a] = whole.astype(BF16)
 
-        @pl.loop(1, 16)
-        def _(t):
+        @pl.loop(6, 21)
+        def _(u):
+            t = lax.rem(u + u // 16, 16)
             push(sum_ref.at[core, a], sum_ref.at[core, a], ssem2.at[10], rsem2.at[10], plane(t)[1])
 
     await_bytes(c2.at[pl.ds(1, 3)], rsem2.at[6])
@@ -447,7 +451,7 @@
     return pl.pallas_call(
         main_kernel,
         out_shape=(
-            jax.ShapeDtypeStruct((16, 64, 256), BF16),
+            jax.ShapeDtypeStruct((64, 16, 256), BF16),
             jax.ShapeDtypeStruct((2, 12, 3, 16, 128), BF16),
             jax.ShapeDtypeStruct((2, 64), F32),
             jax.ShapeDtypeStruct((8, 64), F32),
@@ -462,6 +466,7 @@
             VMEM((2, 64, 128), BF16),
             VMEM((2, 256), F32),
             VMEM((16, 128), BF16),
+            VMEM((16, 64, 256), BF16),
             VMEM((128, 256), F32),
             VMEM((32, 192, 256), BF16),
             VMEM((32, 192, 256), BF16),
@@ -554,7 +559,7 @@
     )
     row_g, col_g, pair, conv, bias, row_f, col_f = finish(sums, own_rows, own_cols, row_w, col_w)
     return (
-        jnp.swapaxes(out_t, 0, 1),
+        out_t,
         row_f,
         col_f,
         row_g.T,

time: 58.6 us -> 56.7 us (0.968)
  Pallas kernels: 54.8 us -> 53.2 us
    pallas_call x1, Pallas kernels: 53.7 us -> 52.1 us  [main(): pl.pallas_call(main_kernel, out_shape=(jax.ShapeDtypeStruct((64, 16, 256)...]
where the time goes in v5:
time: 56.7 us; the launch traced here: 56.6 us
  Pallas kernels  53.2 us (94%)
  local copies, waits for them, and re-layouts  2.67 us (5%)
  between operations  0.76 us (1%)
    pallas_call x1, Pallas kernels, main(): pl.pallas_call(main_kernel, out_shape=(jax.ShapeDtypeStruct((64, 16, 256)...  52.1 us
    unnamed x18, local copies, waits for them, and re-layouts  2.67 us

profile of v5, /device:TPU:1, one launch (start us, length us, event | category | flops | bytes accessed | tf_op | source)
XLA Modules:
  0.0 56.6 jit_solution(8464563831193572378)
XLA Ops:
  0.6 0.0 copy-start
  0.6 0.0 copy-start.1
  0.7 0.0 copy-start.2
  0.7 0.0 copy-start.3
  0.7 0.0 copy-start.4
  0.7 0.0 copy-start.7
  0.7 1.2 %copy.19 = bf16[64,16,256]{2,0,1:T(8,128)(2,1)S(1)} copy(bf16[64,16,256]{2,1,0:T(8,128)(2,1)} %param.17) | data formatting | bytes 1048576 | tf_op args[8]
  1.9 0.0 copy-start.5
  2.0 0.0 copy-start.6
  2.0 0.0 copy-done
  2.0 0.0 copy-done.1
  2.0 0.0 copy-done.2
  2.0 0.0 copy-done.3
  2.0 0.0 copy-done.4
  2.0 0.0 copy-done.7
  2.0 0.6 %copy-done.5 = bf16[2,256]{1,0:T(2,128)(2,1)S(1)} copy-done((bf16[2,256]{1,0:T(2,128)(2,1)S(1)}, bf16[2,256]{1,0:T(2,128)(2,1)}, u32[]{:S(2)}) %copy-start.5) | copy-done | bytes 1048
  2.6 0.0 copy-done.6
  2.6 52.1 %main.1 = (bf16[64,16,256]{2,1,0:T(8,128)(2,1)S(1)}, bf16[2,12,3,16,128]{4,3,2,1,0:T(8,128)(2,1)S(1)}, f32[2,64]{1,0:T(2,128)S(1)}, f32[8,64]{1,0:T(8,128)S(1)}) custom-call(s32[2]{0:T(128)S(1)} %copy-done.6, bf16[2,256]{1,0:T(2,128)(2,1)S(1)} %copy-done.5, bf16[8,256]{1,0:T(8,128)(2,1)S(1)} %copy-done.4, bf16[64,256]{1,0:T(8,128)(2,1)S(1)} %bitcast.12, ...), custom_call_target="tpu_custom_call" | custom-call | tf_op jit(solution)/shard_map/main/pallas_call | solution.py:451
  54.8 1.0 %finish.1 = (f32[64,256]{1,0:T(8,128)}, f32[64,256]{1,0:T(8,128)}, f32[18,64,64]{2,1,0:T(8,128)}, f32[9,64,64]{2,1,0:T(8,128)}, f32[1,64]{1,0:T(1,128)}, /*index=5*/f32[2,256]{1,0:T(2,128)}, f32[8,256]{1,0:T(8,128)}) custom-call(bf16[2,12,3,16,128]{4,3,2,1,0:T(8,128)(2,1)S(1)} %get-tuple-element.20.sums, f32[2,64]{1,0:T(2,128)S(1)} %get-tuple-element.21.drow, ...), custom_call_target="tpu_custom_call" | custom-call | tf_op jit(solution)/shard_map/finish/pallas_call | solution.py:533
  55.8 0.8 %copy.21 = bf16[64,16,256]{2,1,0:T(8,128)(2,1)} copy(bf16[64,16,256]{2,1,0:T(8,128)(2,1)S(1)} %get-tuple-element.38) | data formatting | bytes 1048576
Async XLA Ops:
  0.6 1.3 %copy-start = (bf16[2,3,3,64,64]{4,3,2,1,0:T(8,128)(2,1)S(1)}, bf16[2,3,3,64,64]{4,3,2,1,0:T(8,128)(2,1)}, u32[]{:S(2)}) copy-start(bf16[2,3,3,64,64]{4,3,2,1,0:T(8,128)(2,1)} %pw.1) | copy-start | bytes 442372
  0.6 1.3 %copy-start.1 = (bf16[3,3,64,64]{3,2,1,0:T(8,128)(2,1)S(1)}, bf16[3,3,64,64]{3,2,1,0:T(8,128)(2,1)}, u32[]{:S(2)}) copy-start(bf16[3,3,64,64]{3,2,1,0:T(8,128)(2,1)} %cw.1) | copy-start | bytes 221188
  0.7 1.3 %copy-start.2 = (bf16[256,64]{0,1:T(8,128)(2,1)S(1)}, bf16[256,64]{0,1:T(8,128)(2,1)}, u32[]{:S(2)}) copy-start(bf16[256,64]{0,1:T(8,128)(2,1)} %param.11) | copy-start | bytes 98308
  0.7 1.3 %copy-start.3 = (bf16[256,64]{0,1:T(8,128)(2,1)S(1)}, bf16[256,64]{0,1:T(8,128)(2,1)}, u32[]{:S(2)}) copy-start(bf16[256,64]{0,1:T(8,128)(2,1)} %param.12) | copy-start | bytes 98308
  0.7 1.3 %copy-start.4 = (bf16[8,256]{1,0:T(8,128)(2,1)S(1)}, bf16[8,256]{1,0:T(8,128)(2,1)}, u32[]{:S(2)}) copy-start(bf16[8,256]{1,0:T(8,128)(2,1)} %cf.1) | copy-start | bytes 12292
  0.7 1.3 %copy-start.7 = (f32[64]{0:T(128)S(1)}, f32[64]{0:T(128)}, u32[]{:S(2)}) copy-start(f32[64]{0:T(128)} %param.14) | copy-start | bytes 772
  1.9 0.7 %copy-start.5 = (bf16[2,256]{1,0:T(2,128)(2,1)S(1)}, bf16[2,256]{1,0:T(2,128)(2,1)}, u32[]{:S(2)}) copy-start(bf16[2,256]{1,0:T(2,128)(2,1)} %rf.1) | copy-start | bytes 3076
  2.0 0.7 %copy-start.6 = (s32[2]{0:T(128)S(1)}, s32[2]{0:T(128)}, u32[]{:S(2)}) copy-start(s32[2]{0:T(128)} %dil.1) | copy-start | bytes 28

commit v6 on v5

--- a/solution.py
+++ b/solution.py
@@ -144,8 +144,6 @@
     for slot, r_to in ((2, up), (1, r), (0, down)):
         push(pack.at[0], side.at[1, slot], ssem.at[4], rsem.at[4], (r_to, left))
         push(pack.at[1], side.at[0, slot], ssem.at[4], rsem.at[4], (r_to, right))
-    push(cot.at[pl.ds(8, 8)], halo.at[0], ssem.at[0], rsem.at[0], (down, c))
-    push(cot.at[pl.ds(0, 8)], halo.at[1], ssem.at[1], rsem.at[1], (up, c))
 
     pw0 = jnp.concatenate(
         [jnp.concatenate([pw[0, k, q] for q in range(3)], axis=1) for k in range(3)], axis=0
@@ -193,6 +191,8 @@
     await_bytes(rows.at[1, pl.ds(0, 7)], rsem.at[3])
     push(rows.at[1], rows.at[0], ssem.at[5], rsem.at[5], (down, c))
     push(rows.at[1], rows.at[2], ssem.at[6], rsem.at[6], (up, c))
+    push(cot.at[pl.ds(8, 8)], halo.at[0], ssem.at[0], rsem.at[0], (down, c))
+    push(cot.at[pl.ds(0, 8)], halo.at[1], ssem.at[1], rsem.at[1], (up, c))
     await_bytes(side, rsem.at[4])
     for e in range(8, 24):
         cotangent_row(e)
@@ -258,7 +258,7 @@
         cotangent_row(24 + e)
     live = [1.0 - near[1], None, 1.0 - far[1]]
     rs = [jnp.zeros((64, 128), F32) for _ in range(3)]
-    gc = [jnp.zeros((64, 192), F32) for _ in range(3)]
+    gc = [jnp.zeros((192, 64), F32) for _ in range(3)]
     cs[...] = jnp.zeros((3, 64, 256), F32)
     for i in range(16):
         own = h3[8 + i, 64:128, :]
@@ -266,7 +266,7 @@
         for k in range(3):
             grads = c3[8 + i - (k - 1) * d2]
             d = d + times(wb[k], grads)
-            gc[k] = gc[k] + times_t(own, grads)
+            gc[k] = gc[k] + times_t(grads, own)
         d = d * gs[:, i * 256 : (i + 1) * 256]
         cs[1] = cs[1] + d
         cs[0] = cs[0] + d * jnp.where(row0 + i - d1 >= 0, 1.0, 0.0)
@@ -297,7 +297,7 @@
     bias_g = jnp.broadcast_to(jnp.sum(cs[1], axis=1, keepdims=True), (64, 64)).T
 
     strips = [p0[k * 64 : (k + 1) * 64] for k in range(3)]
-    strips += [p1[q * 64 : (q + 1) * 64] for q in range(3)] + gc
+    strips += [p1[q * 64 : (q + 1) * 64] for q in range(3)] + [part.T for part in gc]
     pairs = [row_proj_g[:, 0:128], row_proj_g[:, 128:256], col_proj_g[:, 0:128], col_proj_g[:, 128:256]]
     pairs += [strip[:, 0:128] for strip in strips]
     rest = [strip[:, 128:192] for strip in strips] + [bias_g]

time: 56.7 us -> 56.2 us (level)
  Pallas kernels: 53.2 us -> 52.6 us
where the time goes in v6:
time: 56.2 us; the launch traced here: 56 us
  Pallas kernels  52.6 us (94%)
  local copies, waits for them, and re-layouts  2.67 us (5%)
  between operations  0.76 us (1%)
    pallas_call x1, Pallas kernels, main(): pl.pallas_call(main_kernel, out_shape=(jax.ShapeDtypeStruct((64, 16, 256)...  51.6 us
    unnamed x18, local copies, waits for them, and re-layouts  2.67 us

profile of v6, /device:TPU:1, one launch (start us, length us, event | category | flops | bytes accessed | tf_op | source)
XLA Modules:
  0.0 56.0 jit_solution(753353859346906136)
XLA Ops:
  0.6 0.0 copy-start
  0.6 0.0 copy-start.1
  0.7 0.0 copy-start.2
  0.7 0.0 copy-start.3
  0.7 0.0 copy-start.4
  0.7 0.0 copy-start.7
  0.7 1.2 %copy.19 = bf16[64,16,256]{2,0,1:T(8,128)(2,1)S(1)} copy(bf16[64,16,256]{2,1,0:T(8,128)(2,1)} %param.17) | data formatting | bytes 1048576 | tf_op args[8]
  1.9 0.0 copy-start.5
  2.0 0.0 copy-start.6
  2.0 0.0 copy-done
  2.0 0.0 copy-done.1
  2.0 0.0 copy-done.2
  2.0 0.0 copy-done.3
  2.0 0.0 copy-done.4
  2.0 0.0 copy-done.7
  2.0 0.6 %copy-done.5 = bf16[2,256]{1,0:T(2,128)(2,1)S(1)} copy-done((bf16[2,256]{1,0:T(2,128)(2,1)S(1)}, bf16[2,256]{1,0:T(2,128)(2,1)}, u32[]{:S(2)}) %copy-start.5) | copy-done | bytes 1048
  2.6 0.0 copy-done.6
  2.6 51.6 %main.1 = (bf16[64,16,256]{2,1,0:T(8,128)(2,1)S(1)}, bf16[2,12,3,16,128]{4,3,2,1,0:T(8,128)(2,1)S(1)}, f32[2,64]{1,0:T(2,128)S(1)}, f32[8,64]{1,0:T(8,128)S(1)}) custom-call(s32[2]{0:T(128)S(1)} %copy-done.6, bf16[2,256]{1,0:T(2,128)(2,1)S(1)} %copy-done.5, bf16[8,256]{1,0:T(8,128)(2,1)S(1)} %copy-done.4, bf16[64,256]{1,0:T(8,128)(2,1)S(1)} %bitcast.12, ...), custom_call_target="tpu_custom_call" | custom-call | tf_op jit(solution)/shard_map/main/pallas_call | solution.py:451
  54.2 1.0 %finish.1 = (f32[64,256]{1,0:T(8,128)}, f32[64,256]{1,0:T(8,128)}, f32[18,64,64]{2,1,0:T(8,128)}, f32[9,64,64]{2,1,0:T(8,128)}, f32[1,64]{1,0:T(1,128)}, /*index=5*/f32[2,256]{1,0:T(2,128)}, f32[8,256]{1,0:T(8,128)}) custom-call(bf16[2,12,3,16,128]{4,3,2,1,0:T(8,128)(2,1)S(1)} %get-tuple-element.20.sums, f32[2,64]{1,0:T(2,128)S(1)} %get-tuple-element.21.drow, ...), custom_call_target="tpu_custom_call" | custom-call | tf_op jit(solution)/shard_map/finish/pallas_call | solution.py:533
  55.3 0.8 %copy.21 = bf16[64,16,256]{2,1,0:T(8,128)(2,1)} copy(bf16[64,16,256]{2,1,0:T(8,128)(2,1)S(1)} %get-tuple-element.38) | data formatting | bytes 1048576
Async XLA Ops:
  0.6 1.3 %copy-start = (bf16[2,3,3,64,64]{4,3,2,1,0:T(8,128)(2,1)S(1)}, bf16[2,3,3,64,64]{4,3,2,1,0:T(8,128)(2,1)}, u32[]{:S(2)}) copy-start(bf16[2,3,3,64,64]{4,3,2,1,0:T(8,128)(2,1)} %pw.1) | copy-start | bytes 442372
  0.6 1.3 %copy-start.1 = (bf16[3,3,64,64]{3,2,1,0:T(8,128)(2,1)S(1)}, bf16[3,3,64,64]{3,2,1,0:T(8,128)(2,1)}, u32[]{:S(2)}) copy-start(bf16[3,3,64,64]{3,2,1,0:T(8,128)(2,1)} %cw.1) | copy-start | bytes 221188
  0.7 1.3 %copy-start.2 = (bf16[256,64]{0,1:T(8,128)(2,1)S(1)}, bf16[256,64]{0,1:T(8,128)(2,1)}, u32[]{:S(2)}) copy-start(bf16[256,64]{0,1:T(8,128)(2,1)} %param.11) | copy-start | bytes 98308
  0.7 1.3 %copy-start.3 = (bf16[256,64]{0,1:T(8,128)(2,1)S(1)}, bf16[256,64]{0,1:T(8,128)(2,1)}, u32[]{:S(2)}) copy-start(bf16[256,64]{0,1:T(8,128)(2,1)} %param.12) | copy-start | bytes 98308
  0.7 1.3 %copy-start.4 = (bf16[8,256]{1,0:T(8,128)(2,1)S(1)}, bf16[8,256]{1,0:T(8,128)(2,1)}, u32[]{:S(2)}) copy-start(bf16[8,256]{1,0:T(8,128)(2,1)} %cf.1) | copy-start | bytes 12292
  0.7 1.3 %copy-start.7 = (f32[64]{0:T(128)S(1)}, f32[64]{0:T(128)}, u32[]{:S(2)}) copy-start(f32[64]{0:T(128)} %param.14) | copy-start | bytes 772
  1.9 0.7 %copy-start.5 = (bf16[2,256]{1,0:T(2,128)(2,1)S(1)}, bf16[2,256]{1,0:T(2,128)(2,1)}, u32[]{:S(2)}) copy-start(bf16[2,256]{1,0:T(2,128)(2,1)} %rf.1) | copy-start | bytes 3076
  2.0 0.7 %copy-start.6 = (s32[2]{0:T(128)S(1)}, s32[2]{0:T(128)}, u32[]{:S(2)}) copy-start(s32[2]{0:T(128)} %dil.1) | copy-start | bytes 28

commit v7 on v6

--- a/solution.py
+++ b/solution.py
@@ -379,7 +379,6 @@
         for k in range(3):
             mixed = mixed + times(wf[k], h3[8 + i + (k - 1) * d2])
         mix[i] = mixed.astype(BF16)
-    out_ref[...] = jnp.swapaxes(mix[...], 0, 1)
 
     @pl.when(a < 12)
     def _():
@@ -394,6 +393,7 @@
             t = lax.rem(u + u // 16, 16)
             push(sum_ref.at[core, a], sum_ref.at[core, a], ssem2.at[10], rsem2.at[10], plane(t)[1])
 
+    out_ref[...] = jnp.swapaxes(mix[...], 0, 1)
     await_bytes(c2.at[pl.ds(1, 3)], rsem2.at[6])
     await_bytes(r2.at[1], rsem2.at[7])
     c2[0] = c1[0, z_hi] + c2[1] + c2[2] + c2[3]

time: 56.2 us -> 56.2 us (level)
  no operation moved by 1% of the time
where the time goes in v7:
time: 56.2 us; the launch traced here: 56 us
  Pallas kernels  52.6 us (94%)
  local copies, waits for them, and re-layouts  2.67 us (5%)
  between operations  0.76 us (1%)
    pallas_call x1, Pallas kernels, main(): pl.pallas_call(main_kernel, out_shape=(jax.ShapeDtypeStruct((64, 16, 256)...  51.6 us
    unnamed x18, local copies, waits for them, and re-layouts  2.67 us

profile of v7, /device:TPU:1, one launch (start us, length us, event | category | flops | bytes accessed | tf_op | source)
XLA Modules:
  0.0 56.0 jit_solution(14705722958802415661)
XLA Ops:
  0.6 0.0 copy-start
  0.6 0.0 copy-start.1
  0.7 0.0 copy-start.2
  0.7 0.0 copy-start.3
  0.7 0.0 copy-start.4
  0.7 0.0 copy-start.7
  0.7 1.2 %copy.19 = bf16[64,16,256]{2,0,1:T(8,128)(2,1)S(1)} copy(bf16[64,16,256]{2,1,0:T(8,128)(2,1)} %param.17) | data formatting | bytes 1048576 | tf_op args[8]
  1.9 0.0 copy-start.5
  2.0 0.0 copy-start.6
  2.0 0.0 copy-done
  2.0 0.0 copy-done.1
  2.0 0.0 copy-done.2
  2.0 0.0 copy-done.3
  2.0 0.0 copy-done.4
  2.0 0.0 copy-done.7
  2.0 0.6 %copy-done.5 = bf16[2,256]{1,0:T(2,128)(2,1)S(1)} copy-done((bf16[2,256]{1,0:T(2,128)(2,1)S(1)}, bf16[2,256]{1,0:T(2,128)(2,1)}, u32[]{:S(2)}) %copy-start.5) | copy-done | bytes 1048
  2.6 0.0 copy-done.6
  2.6 51.6 %main.1 = (bf16[64,16,256]{2,1,0:T(8,128)(2,1)S(1)}, bf16[2,12,3,16,128]{4,3,2,1,0:T(8,128)(2,1)S(1)}, f32[2,64]{1,0:T(2,128)S(1)}, f32[8,64]{1,0:T(8,128)S(1)}) custom-call(s32[2]{0:T(128)S(1)} %copy-done.6, bf16[2,256]{1,0:T(2,128)(2,1)S(1)} %copy-done.5, bf16[8,256]{1,0:T(8,128)(2,1)S(1)} %copy-done.4, bf16[64,256]{1,0:T(8,128)(2,1)S(1)} %bitcast.12, ...), custom_call_target="tpu_custom_call" | custom-call | tf_op jit(solution)/shard_map/main/pallas_call | solution.py:451
  54.2 1.0 %finish.1 = (f32[64,256]{1,0:T(8,128)}, f32[64,256]{1,0:T(8,128)}, f32[18,64,64]{2,1,0:T(8,128)}, f32[9,64,64]{2,1,0:T(8,128)}, f32[1,64]{1,0:T(1,128)}, /*index=5*/f32[2,256]{1,0:T(2,128)}, f32[8,256]{1,0:T(8,128)}) custom-call(bf16[2,12,3,16,128]{4,3,2,1,0:T(8,128)(2,1)S(1)} %get-tuple-element.20.sums, f32[2,64]{1,0:T(2,128)S(1)} %get-tuple-element.21.drow, ...), custom_call_target="tpu_custom_call" | custom-call | tf_op jit(solution)/shard_map/finish/pallas_call | solution.py:533
  55.3 0.8 %copy.21 = bf16[64,16,256]{2,1,0:T(8,128)(2,1)} copy(bf16[64,16,256]{2,1,0:T(8,128)(2,1)S(1)} %get-tuple-element.38) | data formatting | bytes 1048576
Async XLA Ops:
  0.6 1.3 %copy-start = (bf16[2,3,3,64,64]{4,3,2,1,0:T(8,128)(2,1)S(1)}, bf16[2,3,3,64,64]{4,3,2,1,0:T(8,128)(2,1)}, u32[]{:S(2)}) copy-start(bf16[2,3,3,64,64]{4,3,2,1,0:T(8,128)(2,1)} %pw.1) | copy-start | bytes 442372
  0.6 1.3 %copy-start.1 = (bf16[3,3,64,64]{3,2,1,0:T(8,128)(2,1)S(1)}, bf16[3,3,64,64]{3,2,1,0:T(8,128)(2,1)}, u32[]{:S(2)}) copy-start(bf16[3,3,64,64]{3,2,1,0:T(8,128)(2,1)} %cw.1) | copy-start | bytes 221188
  0.7 1.3 %copy-start.2 = (bf16[256,64]{0,1:T(8,128)(2,1)S(1)}, bf16[256,64]{0,1:T(8,128)(2,1)}, u32[]{:S(2)}) copy-start(bf16[256,64]{0,1:T(8,128)(2,1)} %param.11) | copy-start | bytes 98308
  0.7 1.3 %copy-start.3 = (bf16[256,64]{0,1:T(8,128)(2,1)S(1)}, bf16[256,64]{0,1:T(8,128)(2,1)}, u32[]{:S(2)}) copy-start(bf16[256,64]{0,1:T(8,128)(2,1)} %param.12) | copy-start | bytes 98308
  0.7 1.3 %copy-start.4 = (bf16[8,256]{1,0:T(8,128)(2,1)S(1)}, bf16[8,256]{1,0:T(8,128)(2,1)}, u32[]{:S(2)}) copy-start(bf16[8,256]{1,0:T(8,128)(2,1)} %cf.1) | copy-start | bytes 12292
  0.7 1.3 %copy-start.7 = (f32[64]{0:T(128)S(1)}, f32[64]{0:T(128)}, u32[]{:S(2)}) copy-start(f32[64]{0:T(128)} %param.14) | copy-start | bytes 772
  1.9 0.7 %copy-start.5 = (bf16[2,256]{1,0:T(2,128)(2,1)S(1)}, bf16[2,256]{1,0:T(2,128)(2,1)}, u32[]{:S(2)}) copy-start(bf16[2,256]{1,0:T(2,128)(2,1)} %rf.1) | copy-start | bytes 3076
  2.0 0.7 %copy-start.6 = (s32[2]{0:T(128)S(1)}, s32[2]{0:T(128)}, u32[]{:S(2)}) copy-start(s32[2]{0:T(128)} %dil.1) | copy-start | bytes 28
